TPU v7x, 256 devices: a whole 4x4x8 slice. The times are simulated.
256 devices in a mesh: row: 8 (over z_hi, y), col: 32 (over z_lo, x, core).
Axes of the slice: x: 4, y: 4, z: 8 (z_hi: 2, z_lo: 4; z = z_hi * 4 + z_lo), core: 2. Of those that a mesh axis runs over, the one named last changes fastest.
Arguments:
- object_field: float32 [2, 4096, 16384], P(None, 'row', 'col'), may hold values from -6 to 6
- probe_field: float32 [2, 384, 384], replicated, may hold values from -6 to 6
- intensities: bfloat16 [8, 32, 6, 384, 384], P('row', 'col'), may hold values from 0 to 4
- positions: int32 [8, 32, 6, 2], replicated, may hold values from 0 to 511, as said below
- tile_counts: int32 [8, 32], replicated, may hold values from 1 to 6, as said below
Outputs:
- new_object: float32 [2, 4096, 16384], P(None, 'row', 'col')
- new_probe: float32 [2, 384, 384], replicated
Inputs may be any that keep to these rules, and one draw needn't show every extreme that they name: Each entry is a row in 0 to 512 - 1 (first component) or a column in 0 to 512 - 1 (second) of the tile; only slots below the tile's count are scan positions. `tile_counts`: ragged scan positions a tile; some tile holds 6.
All inputs are finite; a program needn't handle non-finite values.
Results may differ from a plain program's by a relative error of at most 0.0061.
The roundings to bfloat16 on the way count: a program that leaves them out, or rounds other values in their place, can miss the bound.
Values may be sent and summed in bfloat16 or wider, within the bound.
No kernel may reach another device: no remote copies, remote signals or barrier semaphores. Data moves between devices by JAX's collectives and lax.ppermute only.
A program may use at most 128 MiB of HBM per device.

v0:
```python
import jax
import jax.numpy as jnp
from jax import lax
from jax.sharding import PartitionSpec as P

OBJECT_REG = 0.1
PROBE_REG = 0.1
PROBE_RATE = 0.5
EPSILON = 1e-06


def passed_along(value, axis, steps):
    count = lax.axis_size(axis)
    initial, last = (max(0, -steps), min(count, count - steps))
    return lax.ppermute(value, axis, [(source, source + steps) for source in range(initial, last)])


def padded(cells, sides, width):
    for axis, dim in sides:
        count = lax.axis_size(axis)
        ends = count - 1
        head = lax.slice_in_dim(cells, 0, width, axis=dim)
        tail = lax.slice_in_dim(cells, cells.shape[dim] - width, cells.shape[dim], axis=dim)
        cells = jnp.concatenate(
            [
                lax.ppermute(tail, axis, [(i, (i + 1) % count) for i in range(ends)]),
                cells,
                lax.ppermute(head, axis, [((i + 1) % count, i) for i in range(ends)]),
            ],
            axis=dim,
        )
    return cells


def dft_tables(length):
    rows_index = lax.iota(jnp.int32, length)
    product = rows_index[:, None] * rows_index[None, :] % length
    angles = product.astype(jnp.float32) * (2.0 * jnp.pi / length)
    norm_factor = 1.0 / jnp.sqrt(jnp.float32(length))
    cos_table = (jnp.cos(angles) * norm_factor).astype(jnp.bfloat16)
    sin_table = (-jnp.sin(angles) * norm_factor).astype(jnp.bfloat16)
    forward_mix = jnp.concatenate(
        [
            jnp.concatenate([cos_table, sin_table], axis=1),
            jnp.concatenate([-sin_table, cos_table], axis=1),
        ],
        axis=0,
    )
    adjoint_mix = jnp.concatenate(
        [
            jnp.concatenate([cos_table, -sin_table], axis=1),
            jnp.concatenate([sin_table, cos_table], axis=1),
        ],
        axis=0,
    )
    return (cos_table, sin_table, forward_mix, adjoint_mix)


def exit_wave(window, probe_field):
    probe_real = probe_field[0]
    probe_imaginary = probe_field[1]
    object_real = window[0]
    object_imaginary = window[1]
    return jnp.concatenate(
        [
            probe_real * object_real - probe_imaginary * object_imaginary,
            probe_real * object_imaginary + probe_imaginary * object_real,
        ],
        axis=1,
    ).astype(jnp.bfloat16)


def wave_gradient(wave_in, intensity, tables):
    cos_table, sin_table, forward_mix, adjoint_mix = tables
    length = cos_table.shape[0]
    cos_part = jnp.dot(cos_table, wave_in, preferred_element_type=jnp.float32)
    sin_part = jnp.dot(sin_table, wave_in, preferred_element_type=jnp.float32)
    halfway = jnp.concatenate(
        [cos_part[:, :length] - sin_part[:, length:], sin_part[:, :length] + cos_part[:, length:]],
        axis=1,
    ).astype(jnp.bfloat16)
    far_field = jnp.dot(halfway, forward_mix, preferred_element_type=jnp.float32)
    far_real = far_field[:, :length]
    far_imaginary = far_field[:, length:]
    misfit = far_real * far_real + far_imaginary * far_imaginary - intensity.astype(jnp.float32)
    residual_wave = jnp.concatenate([misfit * far_real, misfit * far_imaginary], axis=1).astype(
        jnp.bfloat16
    )
    cos_back = jnp.dot(cos_table, residual_wave, preferred_element_type=jnp.float32)
    sin_back = jnp.dot(sin_table, residual_wave, preferred_element_type=jnp.float32)
    returning = jnp.concatenate(
        [cos_back[:, :length] + sin_back[:, length:], cos_back[:, length:] - sin_back[:, :length]],
        axis=1,
    ).astype(jnp.bfloat16)
    return jnp.dot(returning, adjoint_mix, preferred_element_type=jnp.float32)


def deposit_terms(window, probe_field, gradient):
    length = window.shape[1]
    grad_real = gradient[:, :length]
    grad_imaginary = gradient[:, length:]
    probe_real = probe_field[0]
    probe_imaginary = probe_field[1]
    object_real = window[0]
    object_imaginary = window[1]
    object_term = jnp.stack(
        [
            probe_real * grad_real + probe_imaginary * grad_imaginary,
            probe_real * grad_imaginary - probe_imaginary * grad_real,
        ]
    )
    probe_term = jnp.stack(
        [
            object_real * grad_real + object_imaginary * grad_imaginary,
            object_real * grad_imaginary - object_imaginary * grad_real,
            object_real * object_real + object_imaginary * object_imaginary,
        ]
    )
    return (object_term, probe_term)


def add_window(field, corner, update):
    current = lax.dynamic_slice(field, corner, update.shape)
    return lax.dynamic_update_slice(field, current + update, corner)


def fold_columns(accumulated, half_width, tile_width):
    for step_sign in (1, -1):
        outer_rim = (
            accumulated[:, :, tile_width + half_width :]
            if step_sign == 1
            else accumulated[:, :, :half_width]
        )
        arrived = passed_along(outer_rim, "col", step_sign)
        if step_sign == 1:
            accumulated = accumulated.at[:, :, half_width : 2 * half_width].add(arrived)
        else:
            accumulated = accumulated.at[:, :, tile_width : tile_width + half_width].add(arrived)
    return accumulated[:, :, half_width : tile_width + half_width]


def fold_rows(accumulated, half_width, tile_height):
    for step_sign in (1, -1):
        outer_rim = (
            accumulated[:, tile_height + half_width :, :]
            if step_sign == 1
            else accumulated[:, :half_width, :]
        )
        arrived = passed_along(outer_rim, "row", step_sign)
        if step_sign == 1:
            accumulated = accumulated.at[:, half_width : 2 * half_width, :].add(arrived)
        else:
            accumulated = accumulated.at[:, tile_height : tile_height + half_width, :].add(arrived)
    return accumulated[:, half_width : tile_height + half_width, :]


def on_device(object_field, probe_field, intensities, positions, tile_counts):
    tile_height = object_field.shape[1]
    tile_width = object_field.shape[2]
    length = probe_field.shape[1]
    half_width = length // 2
    tables = dft_tables(length)
    row_index = lax.axis_index("row")
    col_index = lax.axis_index("col")
    my_slots = positions[row_index, col_index]
    my_count = tile_counts[row_index, col_index]
    my_intensity = intensities[0, 0]
    probe_power = probe_field[0] * probe_field[0] + probe_field[1] * probe_field[1]
    zero_index = jnp.zeros((), jnp.int32)
    extended = padded(object_field, (("row", 1), ("col", 2)), half_width)
    channels = 3
    accumulated = jnp.zeros((channels, tile_height + length, tile_width + length), jnp.float32)
    probe_sum = jnp.zeros((3, length, length), jnp.float32)

    def window_at(slot_rank):
        return lax.dynamic_slice(
            extended,
            (zero_index, my_slots[slot_rank, 0], my_slots[slot_rank, 1]),
            (2, length, length),
        )

    def deposit(carried, slot_rank, window, gradient):
        field, totals = carried
        object_term, probe_term = deposit_terms(window, probe_field, gradient)
        object_term = jnp.concatenate([object_term, probe_power[None]], axis=0)
        field = add_window(
            field, (zero_index, my_slots[slot_rank, 0], my_slots[slot_rank, 1]), object_term
        )
        return (field, totals + probe_term)

    def own_slot(slot_rank, carried):
        window = window_at(slot_rank)
        gradient = wave_gradient(exit_wave(window, probe_field), my_intensity[slot_rank], tables)
        return deposit(carried, slot_rank, window, gradient)

    carried = lax.fori_loop(0, my_count, own_slot, (accumulated, probe_sum))
    accumulated, probe_sum = carried
    folded = fold_rows(fold_columns(accumulated, half_width, tile_width), half_width, tile_height)
    illumination = folded[2]
    denominator = illumination + OBJECT_REG * jnp.max(probe_power)
    new_object = object_field - folded[:2] / denominator
    probe_total = lax.psum(probe_sum, ("row", "col"))
    probe_denominator = probe_total[2] + PROBE_REG * jnp.max(probe_total[2])
    direction = probe_total[:2] / probe_denominator
    spread = jnp.sqrt(jnp.mean(direction[0] * direction[0] + direction[1] * direction[1]) + EPSILON)
    new_probe = probe_field - PROBE_RATE * direction / spread
    return (new_object, new_probe)


def solution(mesh):
    placed = (P(None, "row", "col"), P(), P("row", "col", None, None, None), P(), P())
    return jax.shard_map(
        on_device,
        mesh=mesh,
        in_specs=placed,
        out_specs=(P(None, "row", "col"), P()),
        check_vma=False,
    )
```

profile of v0, /device:TPU:57, one launch (start us, length us, event | category | flops | bytes accessed | tf_op | source)
XLA Modules:
  0.0 788.4 jit_solution(1636929925284116830)
XLA Ops:
  9.6 7.6 collective-permute-start
  21.1 29.3 %collective-permute-done = f32[2,192,512]{2,1,0:T(8,128)} collective-permute-done((f32[2,192,512]{2,1,0:T(8,128)S(1)}, f32[2,192,512]{2,1,0:T(8,128)}, u32[]{:S(2)}, u32[]{:S(2)}) %collective-permute-start) | collective-permute-done | bytes 786464 | tf_op jit(solution)/shard_map/ppermute | solution.py:26
  51.8 8.9 %collective-permute-done.1 = f32[2,192,512]{2,1,0:T(8,128)} collective-permute-done((f32[2,192,512]{2,1,0:T(8,128)}, f32[2,192,512]{2,1,0:T(8,128)}, u32[]{:S(2)}, u32[]{:S(2)}) %collective-permute-start.1) | collective-permute-done | bytes 786464 | tf_op jit(solution)/shard_map/ppermute | solution.py:28
  91.1 4.9 pad_maximum_fusion.6
  101.6 312.0 %while.18 = (s32[]{:T(128)}, f32[3,896,896]{1,2,0:T(8,128)}, f32[3,384,384]{2,1,0:T(8,128)}, s32[]{:T(128)}, s32[6,2]{0,1:T(2,128)S(1)}, /*index=5*/f32[2,384,38...) while((s32[]{:T(128)}, f32[3,896,896]{1,2,0:T(8,128)}, ...), condition=%wide.region_1.2_spmd.clone.clone, body=%wide.region_0.1_spmd.clone.clone.sunk | while | flops 1834352640 | bytes 75202976 | solution.py:196
  133.3 4.6 maximum_add_fusion.3
  140.2 13.2 %dynamic_update_slice.6 = f32[3,896,896]{1,2,0:T(8,128)} dynamic-update-slice(f32[3,896,896]{1,2,0:T(8,128)} %get-tuple-element.386, f32[3,384,384]{1,2,0:T(8,128)S(1)} %copy.46, s32[]{:T(128)} %constant.144.clone.1..sunk, s32[]{:T(128)S(6)} %select_n.107, s32[]{:T(128)S(6)} %select_n.108) | dynamic-update-slice | bytes 3538948 | tf_op jit(solution)/shard_map/while/body/dynamic_update_slice | solution.py:124
  184.8 4.6 maximum_add_fusion.3
  191.7 13.2 %dynamic_update_slice.6 = f32[3,896,896]{1,2,0:T(8,128)} dynamic-update-slice(f32[3,896,896]{1,2,0:T(8,128)} %get-tuple-element.386, f32[3,384,384]{1,2,0:T(8,128)S(1)} %copy.46, s32[]{:T(128)} %constant.144.clone.1..sunk, s32[]{:T(128)S(6)} %select_n.107, s32[]{:T(128)S(6)} %select_n.108) | dynamic-update-slice | bytes 3538948 | tf_op jit(solution)/shard_map/while/body/dynamic_update_slice | solution.py:124
  236.4 4.6 maximum_add_fusion.3
  243.2 13.8 %dynamic_update_slice.6 = f32[3,896,896]{1,2,0:T(8,128)} dynamic-update-slice(f32[3,896,896]{1,2,0:T(8,128)} %get-tuple-element.386, f32[3,384,384]{1,2,0:T(8,128)S(1)} %copy.46, s32[]{:T(128)} %constant.144.clone.1..sunk, s32[]{:T(128)S(6)} %select_n.107, s32[]{:T(128)S(6)} %select_n.108) | dynamic-update-slice | bytes 3538948 | tf_op jit(solution)/shard_map/while/body/dynamic_update_slice | solution.py:124
  288.5 4.6 maximum_add_fusion.3
  295.4 12.9 %dynamic_update_slice.6 = f32[3,896,896]{1,2,0:T(8,128)} dynamic-update-slice(f32[3,896,896]{1,2,0:T(8,128)} %get-tuple-element.386, f32[3,384,384]{1,2,0:T(8,128)S(1)} %copy.46, s32[]{:T(128)} %constant.144.clone.1..sunk, s32[]{:T(128)S(6)} %select_n.107, s32[]{:T(128)S(6)} %select_n.108) | dynamic-update-slice | bytes 3538948 | tf_op jit(solution)/shard_map/while/body/dynamic_update_slice | solution.py:124
  339.8 4.6 maximum_add_fusion.3
  346.6 13.9 %dynamic_update_slice.6 = f32[3,896,896]{1,2,0:T(8,128)} dynamic-update-slice(f32[3,896,896]{1,2,0:T(8,128)} %get-tuple-element.386, f32[3,384,384]{1,2,0:T(8,128)S(1)} %copy.46, s32[]{:T(128)} %constant.144.clone.1..sunk, s32[]{:T(128)S(6)} %select_n.107, s32[]{:T(128)S(6)} %select_n.108) | dynamic-update-slice | bytes 3538948 | tf_op jit(solution)/shard_map/while/body/dynamic_update_slice | solution.py:124
  392.0 4.6 maximum_add_fusion.3
  398.9 13.8 %dynamic_update_slice.6 = f32[3,896,896]{1,2,0:T(8,128)} dynamic-update-slice(f32[3,896,896]{1,2,0:T(8,128)} %get-tuple-element.386, f32[3,384,384]{1,2,0:T(8,128)S(1)} %copy.46, s32[]{:T(128)} %constant.144.clone.1..sunk, s32[]{:T(128)S(6)} %select_n.107, s32[]{:T(128)S(6)} %select_n.108) | dynamic-update-slice | bytes 3538948 | tf_op jit(solution)/shard_map/while/body/dynamic_update_slice | solution.py:124
  417.3 22.6 %collective-permute-done.4 = f32[3,896,192]{1,2,0:T(8,128)S(1)} collective-permute-done((f32[3,896,192]{1,2,0:T(8,128)S(1)}, f32[3,896,192]{1,2,0:T(8,128)S(1)}, u32[]{:S(2)}, u32[]{:S(2)}) %collective-permute-start.4) | collective-permute-done | bytes 2064416 | tf_op jit(solution)/shard_map/ppermute | solution.py:15
  446.9 26.1 %collective-permute-done.5 = f32[3,896,192]{1,2,0:T(8,128)S(1)} collective-permute-done((f32[3,896,192]{1,2,0:T(8,128)S(1)}, f32[3,896,192]{1,2,0:T(8,128)S(1)}, u32[]{:S(2)}, u32[]{:S(2)}) %collective-permute-start.5) | collective-permute-done | bytes 2064416 | tf_op jit(solution)/shard_map/ppermute | solution.py:15
  481.2 5.4 slice.276
  486.6 10.0 %collective-permute-done.6 = f32[3,192,512]{2,1,0:T(8,128)S(1)} collective-permute-done((f32[3,192,512]{2,1,0:T(8,128)S(1)}, f32[3,192,512]{2,1,0:T(8,128)S(1)}, u32[]{:S(2)}, u32[]{:S(2)}) %collective-permute-start.6) | collective-permute-done | bytes 1179680 | tf_op jit(solution)/shard_map/ppermute | solution.py:15
  499.2 9.1 %scatter-add.16 = f32[3,896,512]{1,2,0:T(8,128)} dynamic-update-slice(f32[3,896,512]{1,2,0:T(8,128)} %slice.276, f32[3,192,512]{1,2,0:T(8,128)S(1)} %slice_add_fusion.4, s32[]{:T(128)} %constant.144.clone.1, s32[]{:T(128)} %constant.154.clone.1, s32[]{:T(128)} %constant.144.clone.1) | dynamic-update-slice | bytes 2359300 | tf_op jit(solution)/shard_map/scatter-add | solution.py:151
  512.3 243.9 %all-reduce.2.cloned.1.call-done = f32[3,384,384]{2,1,0:T(8,128)} async-done(((f32[3,384,384]{2,1,0:T(8,128)}), f32[3,384,384]{2,1,0:T(8,128)}) %all-reduce.2.cloned.1.call-update) | async-done | bytes 1769488 | tf_op jit(solution)/shard_map/psum | solution.py:202
  767.3 8.0 %scatter-add.19 = f32[3,896,512]{1,2,0:T(8,128)} dynamic-update-slice(f32[3,896,512]{1,2,0:T(8,128)} %scatter-add.16, f32[3,192,512]{1,2,0:T(8,128)S(1)} %slice_add_fusion.3, s32[]{:T(128)} %constant.144.clone.1, s32[]{:T(128)} %constant.155.clone.1, s32[]{:T(128)} %constant.144.clone.1) | dynamic-update-slice | bytes 2359300 | tf_op jit(solution)/shard_map/scatter-add | solution.py:153
  (224 shorter events, 257.9 us)
Async XLA Ops:
  7.2 67.3 %copy-start = (s32[8,32,6,2]{1,3,2,0:T(2,128)S(1)}, s32[8,32,6,2]{1,3,2,0:T(2,128)}, u32[]{:S(2)}) copy-start(s32[8,32,6,2]{1,3,2,0:T(2,128)} %param.18) | copy-start | bytes 36868
  7.2 749.0 %all-reduce.2.cloned.1.call-start = ((), (), s32[]{:S(2)}) async-start(), calls=%async_computation | async-start | bytes 3538944 | tf_op jit(solution)/shard_map/psum | solution.py:202
  9.6 40.7 %collective-permute-start = (f32[2,192,512]{2,1,0:T(8,128)S(1)}, f32[2,192,512]{2,1,0:T(8,128)}, u32[]{:S(2)}, u32[]{:S(2)}) collective-permute-start(f32[2,192,512]{2,1,0:T(8,128)S(1)} %get-tuple-element.257), channel_id=1, source_target_pairs={{0,32},{32,64},{64,96},{96,128},{128,160},{160,192},{192,224},{1,3... | collective-permute-start | bytes 2359304 | tf_op jit(solution)/shard_map/ppermute | solution.py:26
  17.2 43.6 %collective-permute-start.1 = (f32[2,192,512]{2,1,0:T(8,128)}, f32[2,192,512]{2,1,0:T(8,128)}, u32[]{:S(2)}, u32[]{:S(2)}) collective-permute-start(f32[2,192,512]{2,1,0:T(8,128)} %get-tuple-element.258), channel_id=1, source_target_pairs={{32,0},{64,32},{96,64},{128,96},{160,128},{192,160},{224,192},{33,... | collective-permute-start | bytes 2359304 | tf_op jit(solution)/shard_map/ppermute | solution.py:28
  21.0 70.1 %copy-start.2 = (f32[2,512,512]{1,2,0:T(8,128)}, f32[2,512,512]{1,2,0:T(8,128)S(1)}, u32[]{:S(2)}) copy-start(f32[2,512,512]{1,2,0:T(8,128)S(1)} %copy.30) | copy-start | bytes 6291460
  51.8 14.9 %copy-start.6 = (f32[2,192,512]{1,2,0:T(8,128)}, f32[2,192,512]{1,2,0:T(8,128)S(1)}, u32[]{:S(2)}) copy-start(f32[2,192,512]{1,2,0:T(8,128)S(1)} %copy.19) | copy-start | bytes 2359300
  66.7 20.0 %collective-permute-start.2 = (f32[2,896,192]{1,2,0:T(8,128)}, f32[2,896,192]{1,2,0:T(8,128)}, u32[]{:S(2)}, u32[]{:S(2)}) collective-permute-start(f32[2,896,192]{1,2,0:T(8,128)} %get-tuple-element.255), channel_id=1, source_target_pairs={{0,1},{1,2},{2,3},{3,4},{4,5},{5,6},{6,7},{7,8},{8,9},{9,10},{10,1... | collective-permute-start | bytes 4128776 | tf_op jit(solution)/shard_map/ppermute | solution.py:26
  71.1 19.9 %collective-permute-start.3 = (f32[2,896,192]{1,2,0:T(8,128)}, f32[2,896,192]{1,2,0:T(8,128)}, u32[]{:S(2)}, u32[]{:S(2)}) collective-permute-start(f32[2,896,192]{1,2,0:T(8,128)} %get-tuple-element.256), channel_id=1, source_target_pairs={{1,0},{2,1},{3,2},{4,3},{5,4},{6,5},{7,6},{8,7},{9,8},{10,9},{11,1... | collective-permute-start | bytes 4128776 | tf_op jit(solution)/shard_map/ppermute | solution.py:28
  81.6 9.5 %copy-start.7 = (f32[2,192,512]{1,2,0:T(8,128)S(1)}, f32[2,192,512]{1,2,0:T(8,128)}, u32[]{:S(2)}) copy-start(f32[2,192,512]{1,2,0:T(8,128)} %copy-done.6) | copy-start | bytes 2359300
  81.6 9.5 %copy-start.8 = (f32[2,192,512]{1,2,0:T(8,128)S(1)}, f32[2,192,512]{1,2,0:T(8,128)}, u32[]{:S(2)}) copy-start(f32[2,192,512]{1,2,0:T(8,128)} %copy.21) | copy-start | bytes 2359300
  102.5 6.8 copy-start.4
  140.2 13.2 %copy-start.5 = (f32[384,384]{1,0:T(8,128)S(1)}, f32[384,384]{1,0:T(8,128)}, u32[]{:S(2)}) copy-start(f32[384,384]{1,0:T(8,128)} %copy-done.4) | copy-start | bytes 1769476 | tf_op jit(solution)/shard_map/while
  154.1 6.8 copy-start.4
  191.7 13.2 %copy-start.5 = (f32[384,384]{1,0:T(8,128)S(1)}, f32[384,384]{1,0:T(8,128)}, u32[]{:S(2)}) copy-start(f32[384,384]{1,0:T(8,128)} %copy-done.4) | copy-start | bytes 1769476 | tf_op jit(solution)/shard_map/while
  205.6 6.8 copy-start.4
  243.2 13.8 %copy-start.5 = (f32[384,384]{1,0:T(8,128)S(1)}, f32[384,384]{1,0:T(8,128)}, u32[]{:S(2)}) copy-start(f32[384,384]{1,0:T(8,128)} %copy-done.4) | copy-start | bytes 1769476 | tf_op jit(solution)/shard_map/while
  257.7 6.8 copy-start.4
  295.4 12.9 %copy-start.5 = (f32[384,384]{1,0:T(8,128)S(1)}, f32[384,384]{1,0:T(8,128)}, u32[]{:S(2)}) copy-start(f32[384,384]{1,0:T(8,128)} %copy-done.4) | copy-start | bytes 1769476 | tf_op jit(solution)/shard_map/while
  346.6 13.9 %copy-start.5 = (f32[384,384]{1,0:T(8,128)S(1)}, f32[384,384]{1,0:T(8,128)}, u32[]{:S(2)}) copy-start(f32[384,384]{1,0:T(8,128)} %copy-done.4) | copy-start | bytes 1769476 | tf_op jit(solution)/shard_map/while
  398.9 13.8 %copy-start.5 = (f32[384,384]{1,0:T(8,128)S(1)}, f32[384,384]{1,0:T(8,128)}, u32[]{:S(2)}) copy-start(f32[384,384]{1,0:T(8,128)} %copy-done.4) | copy-start | bytes 1769476 | tf_op jit(solution)/shard_map/while
  415.4 24.5 %collective-permute-start.4 = (f32[3,896,192]{1,2,0:T(8,128)S(1)}, f32[3,896,192]{1,2,0:T(8,128)S(1)}, u32[]{:S(2)}, u32[]{:S(2)}) collective-permute-start(f32[3,896,192]{1,2,0:T(8,128)S(1)} %slice.216), channel_id=1, source_target_pairs={{0,1},{1,2},{2,3},{3,4},{4,5},{5,6},{6,7},{7,8},{8,9},{9,10},{10,1... | collective-permute-start | bytes 6193160 | tf_op jit(solution)/shard_map/ppermute | solution.py:15
  445.0 28.0 %collective-permute-start.5 = (f32[3,896,192]{1,2,0:T(8,128)S(1)}, f32[3,896,192]{1,2,0:T(8,128)S(1)}, u32[]{:S(2)}, u32[]{:S(2)}) collective-permute-start(f32[3,896,192]{1,2,0:T(8,128)S(1)} %slice.275), channel_id=1, source_target_pairs={{1,0},{2,1},{3,2},{4,3},{5,4},{6,5},{7,6},{8,7},{9,8},{10,9},{11,1... | collective-permute-start | bytes 6193160 | tf_op jit(solution)/shard_map/ppermute | solution.py:15
  478.6 18.0 %collective-permute-start.6 = (f32[3,192,512]{2,1,0:T(8,128)S(1)}, f32[3,192,512]{2,1,0:T(8,128)S(1)}, u32[]{:S(2)}, u32[]{:S(2)}) collective-permute-start(f32[3,192,512]{2,1,0:T(8,128)S(1)} %copy.26), channel_id=1, source_target_pairs={{0,32},{32,64},{64,96},{96,128},{128,160},{160,192},{192,224},{1,3... | collective-permute-start | bytes 3538952 | tf_op jit(solution)/shard_map/ppermute | solution.py:15
  510.3 253.7 %collective-permute-start.7 = (f32[3,192,512]{2,1,0:T(8,128)S(1)}, f32[3,192,512]{2,1,0:T(8,128)}, u32[]{:S(2)}, u32[]{:S(2)}) collective-permute-start(f32[3,192,512]{2,1,0:T(8,128)S(1)} %copy.28), channel_id=1, source_target_pairs={{32,0},{64,32},{96,64},{128,96},{160,128},{192,160},{224,192},{33,... | collective-permute-start | bytes 3538952 | tf_op jit(solution)/shard_map/ppermute | solution.py:15
  (17 other events, 38.7 us)
Sparse Core Ops, SparseCore 0:
  480.7 275.4 all-reduce.1
where the time goes:
time: 796 us; the launch traced here: 788 us
  waiting for transfers between devices  349 us (44%)
  local copies, waits for them, and re-layouts  196 us (25%)
  other arithmetic  105 us (13%)
  matrix products  68.3 us (9%)
  loops' own time  29.9 us (4%)
  starting transfers between devices  23.6 us (3%)
  between operations  16.2 us (2%)
    psum x1, waiting for transfers between devices, on_device(): probe_total = lax.psum(probe_sum, ('row', 'col'))  244 us
    dynamic_update_slice x12, local copies, waits for them, and re-layouts, add_window(): return lax.dynamic_update_slice(field, current + update, corner)  94.2 us
    ppermute x4, waiting for transfers between devices, passed_along(): lax.ppermute(value, axis, [(source, source + steps) for source in range(i...  58.7 us
    ppermute x2, waiting for transfers between devices, padded(): lax.ppermute(tail, axis, [(i, (i + 1) % count) for i in range(ends)])  32.8 us
    another operation x1, loops' own time, on_device(): carried = lax.fori_loop(0, my_count, own_slot, (accumulated, probe_sum))  29.9 us
    add x6, other arithmetic, add_window(): return lax.dynamic_update_slice(field, current + update, corner)  27.7 us
    dynamic_slice x12, local copies, waits for them, and re-layouts, add_window(): current = lax.dynamic_slice(field, corner, update.shape)  20.5 us
    another operation x6, other arithmetic, deposit_terms(): jnp.stack([object_real * grad_real + object_imaginary * grad_imaginary, o...  17.6 us
  transfers between devices with their start and end apart: 9, of which 8 were waited for; matrix products, arithmetic and copies ran while one was open for 5% of the time, Pallas kernels for 0%

commit v1 on v0

v1 whole, which is shorter than its diff:
```python
import functools

import jax
import jax.numpy as jnp
import ml_dtypes
import numpy as np
from jax import lax
from jax.experimental import pallas as pl
from jax.experimental.pallas import tpu as pltpu
from jax.sharding import PartitionSpec as P

OBJECT_REG = 0.1
PROBE_REG = 0.1
PROBE_RATE = 0.5
EPSILON = 1e-06

PS = 384
HALF = 192
TH = 512
TW = 512
PMAX = 6
EH = TH + PS
EW = TW + 512
CANVAS = 1280
TILES = 224
STEP = 32
F32 = jnp.float32
BF16 = jnp.bfloat16


def dft_blocks():
    index = np.arange(PS)
    product = (index[:, None] * index[None, :]) % PS
    angles = product.astype(np.float32) * np.float32(2.0 * np.pi / PS)
    norm = np.float32(1.0) / np.sqrt(np.float32(PS))
    cos = (np.cos(angles) * norm).astype(ml_dtypes.bfloat16)
    sin = (-np.sin(angles) * norm).astype(ml_dtypes.bfloat16)
    forward = np.block([[cos, sin], [-sin, cos]])
    adjoint = np.block([[cos, -sin], [sin, cos]])
    return forward, adjoint


def lane_parts(column):
    block = column // 128
    return block, column - block * 128


def rolled_out(blocks, shift, lanes):
    turned = [pltpu.roll(b, shift, axis=1) for b in blocks]
    keep = lanes >= shift
    zero = jnp.zeros_like(turned[0])
    return [
        jnp.where(keep, turned[0], zero),
        jnp.where(keep, turned[1], turned[0]),
        jnp.where(keep, turned[2], turned[1]),
        jnp.where(keep, zero, turned[2]),
    ]


def rolled_in(blocks, shift, lanes):
    turned = [pltpu.roll(b, (128 - shift) % 128, axis=1) for b in blocks]
    keep = lanes < 128 - shift
    return [jnp.where(keep, turned[k], turned[k + 1]) for k in range(3)]


def illumination_kernel(place, positions, counts, probe, out, canvas, power):
    for k in range(PS // STEP):
        rows = pl.ds(k * STEP, STEP)
        power[rows, :] = probe[0, rows, :] * probe[0, rows, :] + probe[1, rows, :] * probe[1, rows, :]
    for j in range(CANVAS // 128):
        canvas[j, pl.ds(PS, TH), :] = jnp.zeros((TH, 128), F32)
    lanes = lax.broadcasted_iota(jnp.int32, (STEP, 128), 1)
    grid_r, grid_c = 8, 32

    def tile(k, carry):
        down, across = k // 3 - 1, k % 3 - 1
        row, col = place[0] + down, place[1] + across
        inside = (row >= 0) & (row < grid_r) & (col >= 0) & (col < grid_c)
        owner = jnp.where(inside, row * grid_c + col, 0)
        count = jnp.where(inside, counts[owner], 0)

        def slot(s, inner):
            where = (owner * PMAX + s) * 2
            top = positions[where] + down * TH - HALF + PS
            left = positions[where + 1] + across * TW - HALF + PS
            meets = (top > 0) & (top < PS + TH) & (left > 0) & (left < PS + TW)

            @pl.when(meets)
            def _():
                block, shift = lane_parts(left)

                def chunk(c, deep):
                    rows = pl.ds(pl.multiple_of(c * STEP, STEP), STEP)
                    parts = rolled_out([power[rows, pl.ds(j * 128, 128)] for j in range(3)], shift, lanes)
                    for j in range(4):
                        canvas[block + j, pl.ds(top + c * STEP, STEP), :] += parts[j]
                    return deep

                lax.fori_loop(0, PS // STEP, chunk, 0)

            return inner

        return lax.fori_loop(0, count, slot, carry)

    lax.fori_loop(0, 9, tile, 0)
    floor = OBJECT_REG * jnp.max(power[...])
    for j in range(TW // 128):
        out[:, pl.ds(j * 128, 128)] = 1.0 / (canvas[PS // 128 + j, pl.ds(PS, TH), :] + floor)


def main_kernel(
    place, positions, counts, center, above, below, before, after, corners_before, corners_after,
    probe, intensity, forward, adjoint,
    field, rim_before, rim_after, rim_above, rim_below, sums,
    extended, total, wave, halfway, residual, returning, gradient, window, probe_sum,
):
    slots = place[0] * 32 + place[1]
    count = counts[slots]
    lanes = lax.broadcasted_iota(jnp.int32, (STEP, 128), 1)
    total[...] = jnp.zeros_like(total)
    probe_sum[...] = jnp.zeros_like(probe_sum)
    for p in range(2):
        for j in range(EW // 128):
            if 2 <= j < 6:
                middle, cols = center, pl.ds((j - 2) * 128, 128)
                over, under, low = above, below, 0
            else:
                cols = pl.ds(j % 2 * 128, 128)
                middle, over = (before, corners_before) if j < 2 else (after, corners_after)
                under, low = over, HALF
            extended[p, j, pl.ds(0, HALF), :] = over[p, pl.ds(0, HALF), cols].astype(F32)
            extended[p, j, pl.ds(HALF, TH), :] = middle[p, :, cols].astype(F32)
            extended[p, j, pl.ds(HALF + TH, HALF), :] = under[p, pl.ds(low, HALF), cols].astype(F32)

    def slot(s, carry):
        top = positions[(slots * PMAX + s) * 2]
        block, shift = lane_parts(positions[(slots * PMAX + s) * 2 + 1] + 64)

        def leave(c, inner):
            rows = pl.ds(pl.multiple_of(c * STEP, STEP), STEP)
            cells = []
            for p in range(2):
                found = [extended[p, block + j, pl.ds(top + c * STEP, STEP), :] for j in range(4)]
                cells.append(jnp.concatenate(rolled_in(found, shift, lanes), axis=1))
                window[p, rows, :] = cells[p]
            pr, pi = probe[0, rows, :], probe[1, rows, :]
            wave[rows, :] = (pr * cells[0] - pi * cells[1]).astype(BF16)
            wave[pl.ds(pl.multiple_of(PS + c * STEP, STEP), STEP), :] = (pr * cells[1] + pi * cells[0]).astype(BF16)
            return inner

        lax.fori_loop(0, PS // STEP, leave, 0)
        half = jnp.dot(adjoint[...], wave[...], preferred_element_type=F32).astype(BF16)
        halfway[:, pl.ds(0, PS)] = half[:PS]
        halfway[:, pl.ds(PS, PS)] = half[PS:]
        far = jnp.dot(halfway[...], forward[...], preferred_element_type=F32)
        far_r, far_i = far[:, :PS], far[:, PS:]
        misfit = far_r * far_r + far_i * far_i - intensity[s].astype(F32)
        residual[pl.ds(0, PS), :] = (misfit * far_r).astype(BF16)
        residual[pl.ds(PS, PS), :] = (misfit * far_i).astype(BF16)
        back = jnp.dot(forward[...], residual[...], preferred_element_type=F32).astype(BF16)
        returning[:, pl.ds(0, PS)] = back[:PS]
        returning[:, pl.ds(PS, PS)] = back[PS:]
        wave_back = jnp.dot(returning[...], adjoint[...], preferred_element_type=F32)
        gradient[...] = wave_back

        def deposit(c, inner):
            rows = pl.ds(pl.multiple_of(c * STEP, STEP), STEP)
            gr, gi = gradient[rows, pl.ds(0, PS)], gradient[rows, pl.ds(PS, PS)]
            pr, pi = probe[0, rows, :], probe[1, rows, :]
            wr, wi = window[0, rows, :], window[1, rows, :]
            for p, term in ((0, pr * gr + pi * gi), (1, pr * gi - pi * gr)):
                parts = rolled_out([term[:, j * 128 : (j + 1) * 128] for j in range(3)], shift, lanes)
                for j in range(4):
                    total[p, block + j, pl.ds(top + c * STEP, STEP), :] += parts[j]
            probe_sum[0, rows, :] += wr * gr + wi * gi
            probe_sum[1, rows, :] += wr * gi - wi * gr
            probe_sum[2, rows, :] += wr * wr + wi * wi
            return inner

        lax.fori_loop(0, PS // STEP, deposit, 0)
        return carry

    lax.fori_loop(0, count, slot, 0)
    for p in range(2):
        for j in range(EW // 128):
            if 2 <= j < 6:
                cols = pl.ds((j - 2) * 128, 128)
                field[p, :, cols] = total[p, j, pl.ds(HALF, TH), :]
                rim_above[p, :, cols] = total[p, j, pl.ds(0, HALF), :]
                rim_below[p, :, cols] = total[p, j, pl.ds(HALF + TH, HALF), :]
            else:
                rim = rim_before if j < 2 else rim_after
                rim[p, :, pl.ds(j % 2 * 128, 128)] = total[p, j].astype(BF16)
    at = 0
    for p in range(3):
        for k in range(PS // 16):
            for j in range(3):
                sums[at] = probe_sum[p, pl.ds(k * 16, 16), pl.ds(j * 128, 128)].astype(BF16)
                at += 1
    sums[pl.ds(at, TILES - at)] = jnp.zeros((TILES - at, 16, 128), BF16)


def object_kernel(center, field, from_before, from_after, from_above, from_below, weight, out):
    for k in range(TH // 64):
        rows = pl.ds(k * 64, 64)
        outer = pl.ds(HALF + k * 64, 64)
        for p in range(2):
            cells = field[p, rows, :]
            sides = [from_before[p, outer, :], from_after[p, outer, :]]
            cells = cells + jnp.concatenate(sides, axis=1).astype(F32)
            if k * 64 < HALF:
                cells = cells + from_above[p, rows, :].astype(F32)
            if k * 64 >= TH - HALF:
                cells = cells + from_below[p, pl.ds(k * 64 - TH + HALF, 64), :].astype(F32)
            out[p, rows, :] = center[p, rows, :] - cells * weight[rows, :]


def probe_kernel(sums, probe, out, planes):
    at = 0
    for p in range(3):
        for k in range(PS // 16):
            for j in range(3):
                planes[p, pl.ds(k * 16, 16), pl.ds(j * 128, 128)] = sums[at].astype(F32)
                at += 1
    floor = PROBE_REG * jnp.max(planes[2])
    square = jnp.zeros((STEP, PS), F32)
    for k in range(PS // STEP):
        rows = pl.ds(k * STEP, STEP)
        weight = 1.0 / (planes[2, rows, :] + floor)
        for p in range(2):
            direction = planes[p, rows, :] * weight
            planes[p, rows, :] = direction
            square = square + direction * direction
    spread = jnp.sqrt(jnp.sum(square) / (PS * PS) + EPSILON)
    for p in range(2):
        out[p] = probe[p] - PROBE_RATE * planes[p] / spread


SMEM = pl.BlockSpec(memory_space=pltpu.SMEM)
VMEM = pl.BlockSpec(memory_space=pltpu.VMEM)


def params(mib):
    return pltpu.CompilerParams(vmem_limit_bytes=mib << 20)


def shifted(value, axis, step):
    size = lax.axis_size(axis)
    low, high = max(0, -step), min(size, size - step)
    return lax.ppermute(value, axis, [(k, k + step) for k in range(low, high)])


def summed_everywhere(sums):
    core = lax.axis_index("col") % 2
    cols = lax.axis_size("col")
    groups = [list(range(c, cols, 2)) for c in range(2)]
    members = cols // 2
    partner = [(k, k ^ 1) for k in range(cols)]
    halves = sums.reshape(2, TILES // 2, 16, 128)
    kept = lax.dynamic_index_in_dim(halves, core, 0, keepdims=False)
    given = lax.dynamic_index_in_dim(halves, 1 - core, 0, keepdims=False)
    mine = (kept.astype(F32) + lax.ppermute(given, "col", partner).astype(F32)).astype(BF16)
    mine = mine.reshape(members, -1, 16, 128)
    parts = lax.all_to_all(mine, "col", 0, 0, axis_index_groups=groups)
    piece = jnp.sum(parts.astype(F32), axis=0).astype(BF16)
    rows = lax.axis_size("row")
    parts = lax.all_to_all(jnp.broadcast_to(piece[None], (rows,) + piece.shape), "row", 0, 0)
    piece = jnp.sum(parts.astype(F32), axis=0).astype(BF16)
    half = lax.all_to_all(
        jnp.broadcast_to(piece[None], (members,) + piece.shape), "col", 0, 0, axis_index_groups=groups
    ).reshape(TILES // 2, 16, 128)
    other = lax.ppermute(half, "col", partner)
    return jnp.where(core == 0, jnp.concatenate([half, other]), jnp.concatenate([other, half]))


def on_device(object_field, probe_field, intensities, positions, tile_counts):
    place = jnp.stack([lax.axis_index("row"), lax.axis_index("col")]).astype(jnp.int32)
    where = positions.reshape(-1)
    counts = tile_counts.reshape(-1)
    forward, adjoint = dft_blocks()
    rounded = object_field.astype(BF16)
    above = shifted(rounded[:, TH - HALF :, :], "row", 1)
    below = shifted(rounded[:, :HALF, :], "row", -1)
    before = shifted(rounded[:, :, TW - 256 :], "col", 1)
    after = shifted(rounded[:, :, :256], "col", -1)
    weight = pl.pallas_call(
        illumination_kernel,
        out_shape=jax.ShapeDtypeStruct((TH, TW), F32),
        in_specs=[SMEM, SMEM, SMEM, VMEM],
        out_specs=VMEM,
        scratch_shapes=[pltpu.VMEM((CANVAS // 128, CANVAS, 128), F32), pltpu.VMEM((PS, PS), F32)],
        compiler_params=params(24),
        cost_estimate=pl.CostEstimate(flops=20_000_000, bytes_accessed=20_000_000, transcendentals=0),
        name="illumination",
    )(place, where, counts, probe_field)
    corners = jnp.concatenate([above, below], axis=1)
    corners_before = shifted(corners[:, :, TW - 256 :], "col", 1)
    corners_after = shifted(corners[:, :, :256], "col", -1)
    like = jax.ShapeDtypeStruct
    field, rim_before, rim_after, rim_above, rim_below, sums = pl.pallas_call(
        main_kernel,
        out_shape=(
            like((2, TH, TW), F32),
            like((2, EH, 256), BF16),
            like((2, EH, 256), BF16),
            like((2, HALF, TW), F32),
            like((2, HALF, TW), F32),
            like((TILES, 16, 128), BF16),
        ),
        in_specs=[SMEM] * 3 + [VMEM] * 11,
        out_specs=(VMEM,) * 6,
        scratch_shapes=[
            pltpu.VMEM((2, EW // 128, EH, 128), F32),
            pltpu.VMEM((2, EW // 128, EH, 128), F32),
            pltpu.VMEM((2 * PS, PS), BF16),
            pltpu.VMEM((PS, 2 * PS), BF16),
            pltpu.VMEM((2 * PS, PS), BF16),
            pltpu.VMEM((PS, 2 * PS), BF16),
            pltpu.VMEM((PS, 2 * PS), F32),
            pltpu.VMEM((2, PS, PS), F32),
            pltpu.VMEM((3, PS, PS), F32),
        ],
        compiler_params=params(56),
        name="slots",
    )(
        place, where, counts, object_field, above, below, before, after, corners_before, corners_after,
        probe_field, intensities.reshape(PMAX, PS, PS), jnp.asarray(forward), jnp.asarray(adjoint),
    )
    from_before = shifted(rim_after, "col", 1)
    from_after = shifted(rim_before, "col", -1)
    up = rim_above + jnp.concatenate([from_before[:, :HALF], from_after[:, :HALF]], axis=2).astype(F32)
    down = rim_below + jnp.concatenate([from_before[:, HALF + TH :], from_after[:, HALF + TH :]], axis=2).astype(F32)
    from_below = shifted(up.astype(BF16), "row", -1)
    from_above = shifted(down.astype(BF16), "row", 1)
    everywhere = summed_everywhere(sums)
    new_object = pl.pallas_call(
        object_kernel,
        out_shape=like((2, TH, TW), F32),
        in_specs=[VMEM] * 7,
        out_specs=VMEM,
        compiler_params=params(24),
        cost_estimate=pl.CostEstimate(flops=4_000_000, bytes_accessed=12_000_000, transcendentals=0),
        name="new_object",
    )(object_field, field, from_before, from_after, from_above, from_below, weight)
    new_probe = pl.pallas_call(
        probe_kernel,
        out_shape=like((2, PS, PS), F32),
        in_specs=[VMEM] * 2,
        out_specs=VMEM,
        scratch_shapes=[pltpu.VMEM((3, PS, PS), F32)],
        compiler_params=params(24),
        name="new_probe",
    )(everywhere, probe_field)
    return (new_object, new_probe)


def solution(mesh):
    placed = (P(None, "row", "col"), P(), P("row", "col", None, None, None), P(), P())
    return jax.shard_map(
        on_device,
        mesh=mesh,
        in_specs=placed,
        out_specs=(P(None, "row", "col"), P()),
        check_vma=False,
    )
```

time: 796 us -> 187 us (0.23)
  waiting for transfers between devices: 349 us -> 47.9 us
  local copies, waits for them, and re-layouts: 196 us -> 9.52 us
  other arithmetic: 105 us -> 10.2 us
  matrix products: 68.3 us -> 0 us
  starting transfers between devices: 23.6 us -> 74.2 us
  Pallas kernels: 0 us -> 31.4 us
  loops' own time: 29.9 us -> 0 us
  between operations: 16.2 us -> 0.92 us
  blocking collectives: 0 us -> 12.4 us
    psum x1 -> x0, waiting for transfers between devices: 244 us -> none  [on_device(): probe_total = lax.psum(probe_sum, ('row', 'col'))]
    dynamic_update_slice x12 -> x0, local copies, waits for them, and re-layouts: 94.2 us -> none  [add_window(): return lax.dynamic_update_slice(field, current + update, corner)]
    dot_general x36 -> x0, matrix products: 68.3 us -> none  [the longest x6 15.2 us: wave_gradient(): sin_part = jnp.dot(sin_table, wave_in, preferred_element_type=jnp.float32)]
    ppermute x8 -> x12, waiting for transfers between devices: 105 us -> 40.6 us  [the longest x10 39.1 us: shifted(): return lax.ppermute(value, axis, [(k, k + step) for k in range(low, high)])]
    add x14 -> x0, other arithmetic: 36.8 us -> none  [the longest x6 27.7 us: add_window(): return lax.dynamic_update_slice(field, current + update, corner)]
    another operation x30 -> x1, other arithmetic: 34.6 us -> 0.6 us  [on_device(): jnp.stack([lax.axis_index('row'), lax.axis_index('col')]).astype(jnp.int32)]
    pallas_call x0 -> x4, Pallas kernels: none -> 31.4 us  [the longest x1 18.6 us: on_device(): pl.pallas_call(main_kernel, out_shape=(like((2, TH, TW), F32), like((2, E...]
    all_to_all x0 -> x2, starting transfers between devices: none -> 31.4 us  [the longest x1 25.9 us: summed_everywhere(): parts = lax.all_to_all(mine, 'col', 0, 0, axis_index_groups=groups)]
  transfers between devices with their start and end apart: 9 -> 14, of which waited for: 8 -> 8; matrix products, arithmetic and copies ran while one was open for 5% -> 6% of each run, Pallas kernels for 0% -> 6%
where the time goes in v1:
time: 187 us
  starting transfers between devices  74.2 us (40%)
  waiting for transfers between devices  47.9 us (26%)
  Pallas kernels  31.4 us (17%)
  blocking collectives  12.4 us (7%)
  other arithmetic  10.2 us (5%)
  local copies, waits for them, and re-layouts  9.52 us (5%)
    ppermute x10, waiting for transfers between devices, shifted(): return lax.ppermute(value, axis, [(k, k + step) for k in range(low, high)])  39.1 us
    ppermute x10, starting transfers between devices, shifted(): return lax.ppermute(value, axis, [(k, k + step) for k in range(low, high)])  37.5 us
    all_to_all x1, starting transfers between devices, summed_everywhere(): parts = lax.all_to_all(mine, 'col', 0, 0, axis_index_groups=groups)  25.9 us
    pallas_call x1, Pallas kernels, on_device(): pl.pallas_call(main_kernel, out_shape=(like((2, TH, TW), F32), like((2, E...  18.6 us
    all_to_all x1, blocking collectives, summed_everywhere(): lax.all_to_all(jnp.broadcast_to(piece[None], (rows,) + piece.shape), 'row...  12.4 us
    pallas_call x1, Pallas kernels, on_device(): pl.pallas_call(illumination_kernel, out_shape=jax.ShapeDtypeStruct((TH, T...  8.13 us
    all_to_all x1, waiting for transfers between devices, summed_everywhere(): parts = lax.all_to_all(mine, 'col', 0, 0, axis_index_groups=groups)  7.33 us
    all_to_all x1, starting transfers between devices, summed_everywhere(): lax.all_to_all(jnp.broadcast_to(piece[None], (members,) + piece.shape), '...  5.5 us
  transfers between devices with their start and end apart: 14, of which 8 were waited for; matrix products, arithmetic and copies ran while one was open for 6% of the time, Pallas kernels for 6%

profile of v1, /device:TPU:57, one launch (start us, length us, event | category | flops | bytes accessed | tf_op | source)
XLA Modules:
  0.0 186.7 jit_solution(17615441798083545072)
XLA Ops:
  2.4 7.6 %collective-permute-start = (bf16[2,192,512]{2,1,0:T(8,128)(2,1)S(1)}, bf16[2,192,512]{2,1,0:T(8,128)(2,1)S(1)}, u32[]{:S(2)}, u32[]{:S(2)}) collective-permute-start(bf16[2,192,512]{2,1,0:T(8,128)(2,1)S(1)} %get-tuple-element.17), channel_id=1, source_target_pairs={{0,32},{32,64},{64,96},{96,128},{128,160},{160,192},{192,224},{1,3... | collective-permute-start | bytes 1179656 | tf_op jit(solution)/shard_map/ppermute | solution.py:250
  10.0 1.9 %collective-permute-start.1 = (bf16[2,192,512]{2,1,0:T(8,128)(2,1)S(1)}, bf16[2,192,512]{2,1,0:T(8,128)(2,1)S(1)}, u32[]{:S(2)}, u32[]{:S(2)}) collective-permute-start(bf16[2,192,512]{2,1,0:T(8,128)(2,1)S(1)} %get-tuple-element.16), channel_id=1, source_target_pairs={{32,0},{64,32},{96,64},{128,96},{160,128},{192,160},{224,192},{33,... | collective-permute-start | bytes 1179656 | tf_op jit(solution)/shard_map/ppermute | solution.py:250
  12.8 4.1 %collective-permute-start.2 = (bf16[2,512,256]{2,1,0:T(8,128)(2,1)}, bf16[2,512,256]{2,1,0:T(8,128)(2,1)S(1)}, u32[]{:S(2)}, u32[]{:S(2)}) collective-permute-start(bf16[2,512,256]{2,1,0:T(8,128)(2,1)} %get-tuple-element.15), channel_id=1, source_target_pairs={{0,1},{1,2},{2,3},{3,4},{4,5},{5,6},{6,7},{7,8},{8,9},{9,10},{10,1... | collective-permute-start | bytes 1572872 | tf_op jit(solution)/shard_map/ppermute | solution.py:250
  16.9 1.9 %collective-permute-start.3 = (bf16[2,512,256]{2,1,0:T(8,128)(2,1)S(1)}, bf16[2,512,256]{2,1,0:T(8,128)(2,1)S(1)}, u32[]{:S(2)}, u32[]{:S(2)}) collective-permute-start(bf16[2,512,256]{2,1,0:T(8,128)(2,1)S(1)} %get-tuple-element.14), channel_id=1, source_target_pairs={{1,0},{2,1},{3,2},{4,3},{5,4},{6,5},{7,6},{8,7},{9,8},{10,9},{11,1... | collective-permute-start | bytes 1572872 | tf_op jit(solution)/shard_map/ppermute | solution.py:250
  18.8 7.5 %collective-permute-done.above = bf16[2,192,512]{2,1,0:T(8,128)(2,1)S(1)} collective-permute-done((bf16[2,192,512]{2,1,0:T(8,128)(2,1)S(1)}, bf16[2,192,512]{2,1,0:T(8,128)(2,1)S(1)}, u32[]{:S(2)}, u32[]{:S(2)}) %collective-permute-start) | collective-permute-done | bytes 393248 | tf_op jit(solution)/shard_map/ppermute | solution.py:250
  26.4 10.1 %collective-permute-done.1.below = bf16[2,192,512]{2,1,0:T(8,128)(2,1)S(1)} collective-permute-done((bf16[2,192,512]{2,1,0:T(8,128)(2,1)S(1)}, bf16[2,192,512]{2,1,0:T(8,128)(2,1)S(1)}, u32[]{:S(2)}, u32[]{:S(2)}) %collective-permute-start.1) | collective-permute-done | bytes 393248 | tf_op jit(solution)/shard_map/ppermute | solution.py:250
  37.4 4.5 %collective-permute-start.4 = (bf16[2,384,256]{2,1,0:T(8,128)(2,1)}, bf16[2,384,256]{2,1,0:T(8,128)(2,1)}, u32[]{:S(2)}, u32[]{:S(2)}) collective-permute-start(bf16[2,384,256]{2,1,0:T(8,128)(2,1)} %get-tuple-element.23), channel_id=1, source_target_pairs={{0,1},{1,2},{2,3},{3,4},{4,5},{5,6},{6,7},{7,8},{8,9},{9,10},{10,1... | collective-permute-start | bytes 1179656 | tf_op jit(solution)/shard_map/ppermute | solution.py:250
  41.9 1.9 %collective-permute-start.5 = (bf16[2,384,256]{2,1,0:T(8,128)(2,1)}, bf16[2,384,256]{2,1,0:T(8,128)(2,1)}, u32[]{:S(2)}, u32[]{:S(2)}) collective-permute-start(bf16[2,384,256]{2,1,0:T(8,128)(2,1)} %get-tuple-element.22), channel_id=1, source_target_pairs={{1,0},{2,1},{3,2},{4,3},{5,4},{6,5},{7,6},{8,7},{9,8},{10,9},{11,1... | collective-permute-start | bytes 1179656 | tf_op jit(solution)/shard_map/ppermute | solution.py:250
  46.9 4.4 %collective-permute-done.5.corners_after = bf16[2,384,256]{2,1,0:T(8,128)(2,1)} collective-permute-done((bf16[2,384,256]{2,1,0:T(8,128)(2,1)}, bf16[2,384,256]{2,1,0:T(8,128)(2,1)}, u32[]{:S(2)}, u32[]{:S(2)}) %collective-permute-start.5) | collective-permute-done | bytes 393248 | tf_op jit(solution)/shard_map/ppermute | solution.py:250
  51.3 18.6 %slots.1 = (f32[2,512,512]{2,1,0:T(8,128)}, bf16[2,896,256]{2,1,0:T(8,128)(2,1)}, bf16[2,896,256]{2,1,0:T(8,128)(2,1)}, f32[2,192,512]{2,1,0:T(8,128)}, f32[2,19...) custom-call(s32[2]{0:T(128)} %pad_add_fusion.place, s32[3072]{0:T(1024)} %reshape.26.positions, s32[256]{0:T(256)} %reshape.27.counts, ...), custom_call_target="tpu_custom_call" | custom-call | tf_op jit(solution)/shard_map/slots/pallas_call | solution.py:300
  75.5 25.9 %all-to-all-start = ((bf16[16,7,16,128]{3,2,1,0:T(8,128)(2,1)}), bf16[16,7,16,128]{3,2,1,0:T(8,128)(2,1)S(1)}, u32[]{:S(2)}, u32[]{:S(2)}) async-start(bf16[16,7,16,128]{3,2,1,0:T(8,128)(2,1)} %bitcast.6), calls=%async_computation | async-start | bytes 917504 | tf_op jit(solution)/shard_map/all_to_all | solution.py:264
  101.4 2.6 %collective-permute-start.7 = (bf16[2,896,256]{2,1,0:T(8,128)(2,1)}, bf16[2,896,256]{2,1,0:T(8,128)(2,1)S(1)}, u32[]{:S(2)}, u32[]{:S(2)}) collective-permute-start(bf16[2,896,256]{2,1,0:T(8,128)(2,1)} %get-tuple-element.10), channel_id=1, source_target_pairs={{1,0},{2,1},{3,2},{4,3},{5,4},{6,5},{7,6},{8,7},{9,8},{10,9},{11,1... | collective-permute-start | bytes 2752520 | tf_op jit(solution)/shard_map/ppermute | solution.py:250
  104.0 3.0 %collective-permute-start.6 = (bf16[2,896,256]{2,1,0:T(8,128)(2,1)S(1)}, bf16[2,896,256]{2,1,0:T(8,128)(2,1)S(1)}, u32[]{:S(2)}, u32[]{:S(2)}) collective-permute-start(bf16[2,896,256]{2,1,0:T(8,128)(2,1)S(1)} %copy-done.16), channel_id=1, source_target_pairs={{0,1},{1,2},{2,3},{3,4},{4,5},{5,6},{6,7},{7,8},{8,9},{9,10},{10,1... | collective-permute-start | bytes 2752520 | tf_op jit(solution)/shard_map/ppermute | solution.py:250
  107.0 7.3 %all-to-all-done = bf16[16,7,16,128]{3,2,1,0:T(8,128)(2,1)S(1)} async-done(((bf16[16,7,16,128]{3,2,1,0:T(8,128)(2,1)}), bf16[16,7,16,128]{3,2,1,0:T(8,128)(2,1)S(1)}, u32[]{:S(2)}, u32[]{:S(2)}) %all-to-all-start) | async-done | bytes 458784 | tf_op jit(solution)/shard_map/all_to_all | solution.py:264
  114.4 12.4 %all_to_all.15 = bf16[8,7,16,128]{3,2,1,0:T(8,128)(2,1)S(1)} all-to-all(bf16[8,7,16,128]{3,2,1,0:T(8,128)(2,1)S(1)} %broadcast_in_dim.4), channel_id=1, replica_groups=mesh['row'=8,'col'=32] {'row'}, dimensions={0} | all-to-all | bytes 458752 | tf_op jit(solution)/shard_map/all_to_all | solution.py:267
  127.8 5.5 %all-to-all-start.2 = ((bf16[16,7,16,128]{3,2,1,0:T(8,128)(2,1)}), bf16[16,7,16,128]{3,2,1,0:T(8,128)(2,1)}, u32[]{:S(2)}, u32[]{:S(2)}) async-start(bf16[16,7,16,128]{3,2,1,0:T(8,128)(2,1)} %broadcast_in_dim.5), calls=%async_computation.2 | async-start | bytes 917504 | tf_op jit(solution)/shard_map/all_to_all | solution.py:269
  134.1 2.1 %add_convert_fusion.1 = bf16[2,192,512]{2,1,0:T(8,128)(2,1)} fusion(f32[2,192,512]{2,1,0:T(8,128)} %get-tuple-element.11, bf16[2,192,256]{2,1,0:T(8,128)(2,1)S(1)} %get-tuple-element.21, bf16[2,192,256]{2,1,0:T(8,128)(2,1)S(1)} %get-tuple-element.19), kind=kLoop, calls=%fused_computation.4 | loop fusion | flops 1179648 | bytes 1572864 | tf_op jit(solution)/shard_map/convert_element_type | solution.py:334
  136.2 7.6 %collective-permute-start.8 = (bf16[2,192,512]{2,1,0:T(8,128)(2,1)}, bf16[2,192,512]{2,1,0:T(8,128)(2,1)}, u32[]{:S(2)}, u32[]{:S(2)}) collective-permute-start(bf16[2,192,512]{2,1,0:T(8,128)(2,1)} %add_convert_fusion.1), channel_id=1, source_target_pairs={{0,32},{32,64},{64,96},{96,128},{128,160},{160,192},{192,224},{1,3... | collective-permute-start | bytes 1179656 | tf_op jit(solution)/shard_map/ppermute | solution.py:250
  143.8 4.2 %collective-permute-start.11 = (bf16[112,16,128]{2,1,0:T(8,128)(2,1)}, bf16[112,16,128]{2,1,0:T(8,128)(2,1)}, u32[]{:S(2)}, u32[]{:S(2)}) collective-permute-start(bf16[112,16,128]{2,1,0:T(8,128)(2,1)} %bitcast.7), channel_id=1, source_target_pairs={{0,1},{1,0},{2,3},{3,2},{4,5},{5,4},{6,7},{7,6},{8,9},{9,8},{10,11... | collective-permute-start | bytes 1376264 | tf_op jit(solution)/shard_map/ppermute | solution.py:272
  148.0 2.2 %add_convert_fusion = bf16[2,192,512]{2,1,0:T(8,128)(2,1)} fusion(f32[2,192,512]{2,1,0:T(8,128)} %get-tuple-element.12, bf16[2,192,256]{2,1,0:T(8,128)(2,1)S(1)} %get-tuple-element.20, bf16[2,192,256]{2,1,0:T(8,128)(2,1)} %get-tuple-element.18), kind=kLoop, calls=%fused_computation.3 | loop fusion | flops 1179648 | bytes 1572864 | tf_op jit(solution)/shard_map/convert_element_type | solution.py:333
  150.2 2.5 %collective-permute-start.9 = (bf16[2,192,512]{2,1,0:T(8,128)(2,1)}, bf16[2,192,512]{2,1,0:T(8,128)(2,1)}, u32[]{:S(2)}, u32[]{:S(2)}) collective-permute-start(bf16[2,192,512]{2,1,0:T(8,128)(2,1)} %add_convert_fusion), channel_id=1, source_target_pairs={{32,0},{64,32},{96,64},{128,96},{160,128},{192,160},{224,192},{33,... | collective-permute-start | bytes 1179656 | tf_op jit(solution)/shard_map/ppermute | solution.py:250
  152.8 8.1 %illumination.1.weight = f32[512,512]{1,0:T(8,128)S(1)} custom-call(s32[2]{0:T(128)S(1)} %copy-done.9, s32[3072]{0:T(1024)S(1)} %copy-done.7, s32[256]{0:T(256)S(1)} %copy-done.8, f32[2,384,384]{2,1,0:T(8,128)S(1)} %copy-done.1), custom_call_target="tpu_custom_call" | custom-call | flops 20000000 | bytes 20000000 | tf_op jit(solution)/shard_map/illumination/pallas_call | solution.py:286
  161.2 16.3 %collective-permute-done.9.from_below = bf16[2,192,512]{2,1,0:T(8,128)(2,1)} collective-permute-done((bf16[2,192,512]{2,1,0:T(8,128)(2,1)}, bf16[2,192,512]{2,1,0:T(8,128)(2,1)}, u32[]{:S(2)}, u32[]{:S(2)}) %collective-permute-start.9) | collective-permute-done | bytes 393248 | tf_op jit(solution)/shard_map/ppermute | solution.py:250
  180.4 2.8 %new_object.1 = f32[2,512,512]{2,1,0:T(8,128)} custom-call(f32[2,512,512]{2,1,0:T(8,128)S(1)} %copy-done, f32[2,512,512]{2,1,0:T(8,128)S(1)} %copy-done.2, bf16[2,896,256]{2,1,0:T(8,128)(2,1)S(1)} %copy-done.6, bf16[2,896,256]{2,1,0:T(8,128)(2,1)S(1)} %copy-done.4, bf16[2,192,512]{2,1,0:T(8,128)(2,1)} %collective-permute-done.8.from_above, ...), custom_call_target="tpu_custom_call" | custom-call | flops 4000000 | bytes 12000000 | tf_op jit(solution)/shard_map/new_object/pallas_call | solution.py:336
  (64 shorter events, 20.7 us)
Async XLA Ops:
  2.4 23.9 %collective-permute-start = (bf16[2,192,512]{2,1,0:T(8,128)(2,1)S(1)}, bf16[2,192,512]{2,1,0:T(8,128)(2,1)S(1)}, u32[]{:S(2)}, u32[]{:S(2)}) collective-permute-start(bf16[2,192,512]{2,1,0:T(8,128)(2,1)S(1)} %get-tuple-element.17), channel_id=1, source_target_pairs={{0,32},{32,64},{64,96},{96,128},{128,160},{160,192},{192,224},{1,3... | collective-permute-start | bytes 1179656 | tf_op jit(solution)/shard_map/ppermute | solution.py:250
  10.0 26.4 %collective-permute-start.1 = (bf16[2,192,512]{2,1,0:T(8,128)(2,1)S(1)}, bf16[2,192,512]{2,1,0:T(8,128)(2,1)S(1)}, u32[]{:S(2)}, u32[]{:S(2)}) collective-permute-start(bf16[2,192,512]{2,1,0:T(8,128)(2,1)S(1)} %get-tuple-element.16), channel_id=1, source_target_pairs={{32,0},{64,32},{96,64},{128,96},{160,128},{192,160},{224,192},{33,... | collective-permute-start | bytes 1179656 | tf_op jit(solution)/shard_map/ppermute | solution.py:250
  12.8 31.0 %copy-start.14 = (s32[8,32,6,2]{1,3,2,0:T(2,128)S(1)}, s32[8,32,6,2]{1,3,2,0:T(2,128)}, u32[]{:S(2)}) copy-start(s32[8,32,6,2]{1,3,2,0:T(2,128)} %param.10) | copy-start | bytes 36868
  12.8 33.6 %collective-permute-start.2 = (bf16[2,512,256]{2,1,0:T(8,128)(2,1)}, bf16[2,512,256]{2,1,0:T(8,128)(2,1)S(1)}, u32[]{:S(2)}, u32[]{:S(2)}) collective-permute-start(bf16[2,512,256]{2,1,0:T(8,128)(2,1)} %get-tuple-element.15), channel_id=1, source_target_pairs={{0,1},{1,2},{2,3},{3,4},{4,5},{5,6},{6,7},{7,8},{8,9},{9,10},{10,1... | collective-permute-start | bytes 1572872 | tf_op jit(solution)/shard_map/ppermute | solution.py:250
  16.9 29.5 %collective-permute-start.3 = (bf16[2,512,256]{2,1,0:T(8,128)(2,1)S(1)}, bf16[2,512,256]{2,1,0:T(8,128)(2,1)S(1)}, u32[]{:S(2)}, u32[]{:S(2)}) collective-permute-start(bf16[2,512,256]{2,1,0:T(8,128)(2,1)S(1)} %get-tuple-element.14), channel_id=1, source_target_pairs={{1,0},{2,1},{3,2},{4,3},{5,4},{6,5},{7,6},{8,7},{9,8},{10,9},{11,1... | collective-permute-start | bytes 1572872 | tf_op jit(solution)/shard_map/ppermute | solution.py:250
  26.3 18.0 %copy-start.10 = (bf16[2,192,512]{2,1,0:T(8,128)(2,1)}, bf16[2,192,512]{2,1,0:T(8,128)(2,1)S(1)}, u32[]{:S(2)}) copy-start(bf16[2,192,512]{2,1,0:T(8,128)(2,1)S(1)} %collective-permute-done.above) | copy-start | bytes 1179652
  37.4 9.5 %collective-permute-start.4 = (bf16[2,384,256]{2,1,0:T(8,128)(2,1)}, bf16[2,384,256]{2,1,0:T(8,128)(2,1)}, u32[]{:S(2)}, u32[]{:S(2)}) collective-permute-start(bf16[2,384,256]{2,1,0:T(8,128)(2,1)} %get-tuple-element.23), channel_id=1, source_target_pairs={{0,1},{1,2},{2,3},{3,4},{4,5},{5,6},{6,7},{7,8},{8,9},{9,10},{10,1... | collective-permute-start | bytes 1179656 | tf_op jit(solution)/shard_map/ppermute | solution.py:250
  41.9 9.4 %collective-permute-start.5 = (bf16[2,384,256]{2,1,0:T(8,128)(2,1)}, bf16[2,384,256]{2,1,0:T(8,128)(2,1)}, u32[]{:S(2)}, u32[]{:S(2)}) collective-permute-start(bf16[2,384,256]{2,1,0:T(8,128)(2,1)} %get-tuple-element.22), channel_id=1, source_target_pairs={{1,0},{2,1},{3,2},{4,3},{5,4},{6,5},{7,6},{8,7},{9,8},{10,9},{11,1... | collective-permute-start | bytes 1179656 | tf_op jit(solution)/shard_map/ppermute | solution.py:250
  69.9 34.0 %copy-start.16 = (bf16[2,896,256]{2,1,0:T(8,128)(2,1)S(1)}, bf16[2,896,256]{2,1,0:T(8,128)(2,1)}, u32[]{:S(2)}) copy-start(bf16[2,896,256]{2,1,0:T(8,128)(2,1)} %get-tuple-element.9) | copy-start | bytes 2752516
  71.1 2.5 %collective-permute-start.10 = (bf16[112,16,128]{2,1,0:T(8,128)(2,1)S(1)}, bf16[112,16,128]{2,1,0:T(8,128)(2,1)S(1)}, u32[]{:S(2)}, u32[]{:S(2)}) collective-permute-start(bf16[112,16,128]{2,1,0:T(8,128)(2,1)S(1)} %dynamic-slice_bitcast_fusion), channel_id=1, source_target_pairs={{0,1},{1,0},{2,3},{3,2},{4,5},{5,4},{6,7},{7,6},{8,9},{9,8},{10,11... | collective-permute-start | bytes 1376264 | tf_op jit(solution)/shard_map/ppermute | solution.py:262
  75.5 38.9 %all-to-all-start = ((bf16[16,7,16,128]{3,2,1,0:T(8,128)(2,1)}), bf16[16,7,16,128]{3,2,1,0:T(8,128)(2,1)S(1)}, u32[]{:S(2)}, u32[]{:S(2)}) async-start(bf16[16,7,16,128]{3,2,1,0:T(8,128)(2,1)} %bitcast.6), calls=%async_computation | async-start | bytes 917504 | tf_op jit(solution)/shard_map/all_to_all | solution.py:264
  101.4 31.9 %collective-permute-start.7 = (bf16[2,896,256]{2,1,0:T(8,128)(2,1)}, bf16[2,896,256]{2,1,0:T(8,128)(2,1)S(1)}, u32[]{:S(2)}, u32[]{:S(2)}) collective-permute-start(bf16[2,896,256]{2,1,0:T(8,128)(2,1)} %get-tuple-element.10), channel_id=1, source_target_pairs={{1,0},{2,1},{3,2},{4,3},{5,4},{6,5},{7,6},{8,7},{9,8},{10,9},{11,1... | collective-permute-start | bytes 2752520 | tf_op jit(solution)/shard_map/ppermute | solution.py:250
  104.0 29.3 %collective-permute-start.6 = (bf16[2,896,256]{2,1,0:T(8,128)(2,1)S(1)}, bf16[2,896,256]{2,1,0:T(8,128)(2,1)S(1)}, u32[]{:S(2)}, u32[]{:S(2)}) collective-permute-start(bf16[2,896,256]{2,1,0:T(8,128)(2,1)S(1)} %copy-done.16), channel_id=1, source_target_pairs={{0,1},{1,2},{2,3},{3,4},{4,5},{5,6},{6,7},{7,8},{8,9},{9,10},{10,1... | collective-permute-start | bytes 2752520 | tf_op jit(solution)/shard_map/ppermute | solution.py:250
  127.8 16.1 %all-to-all-start.2 = ((bf16[16,7,16,128]{3,2,1,0:T(8,128)(2,1)}), bf16[16,7,16,128]{3,2,1,0:T(8,128)(2,1)}, u32[]{:S(2)}, u32[]{:S(2)}) async-start(bf16[16,7,16,128]{3,2,1,0:T(8,128)(2,1)} %broadcast_in_dim.5), calls=%async_computation.2 | async-start | bytes 917504 | tf_op jit(solution)/shard_map/all_to_all | solution.py:269
  133.3 14.8 %copy-start.3 = (bf16[2,896,256]{2,1,0:T(8,128)(2,1)}, bf16[2,896,256]{2,1,0:T(8,128)(2,1)S(1)}, u32[]{:S(2)}) copy-start(bf16[2,896,256]{2,1,0:T(8,128)(2,1)S(1)} %collective-permute-done.7.from_after) | copy-start | bytes 2752516
  134.1 18.6 %copy-start.1 = (f32[2,384,384]{2,1,0:T(8,128)S(1)}, f32[2,384,384]{2,1,0:T(8,128)}, u32[]{:S(2)}) copy-start(f32[2,384,384]{2,1,0:T(8,128)} %probe.5) | copy-start | bytes 3538948
  134.1 18.6 %copy-start.7 = (s32[3072]{0:T(1024)S(1)}, s32[3072]{0:T(1024)}, u32[]{:S(2)}) copy-start(s32[3072]{0:T(1024)} %reshape.26.positions) | copy-start | bytes 36868
  134.1 18.6 %copy-start.8 = (s32[256]{0:T(256)S(1)}, s32[256]{0:T(256)}, u32[]{:S(2)}) copy-start(s32[256]{0:T(256)} %reshape.27.counts) | copy-start | bytes 3076
  134.1 18.6 %copy-start.9 = (s32[2]{0:T(128)S(1)}, s32[2]{0:T(128)}, u32[]{:S(2)}) copy-start(s32[2]{0:T(128)} %pad_add_fusion.place) | copy-start | bytes 28
  136.2 25.0 %collective-permute-start.8 = (bf16[2,192,512]{2,1,0:T(8,128)(2,1)}, bf16[2,192,512]{2,1,0:T(8,128)(2,1)}, u32[]{:S(2)}, u32[]{:S(2)}) collective-permute-start(bf16[2,192,512]{2,1,0:T(8,128)(2,1)} %add_convert_fusion.1), channel_id=1, source_target_pairs={{0,32},{32,64},{64,96},{96,128},{128,160},{160,192},{192,224},{1,3... | collective-permute-start | bytes 1179656 | tf_op jit(solution)/shard_map/ppermute | solution.py:250
  143.8 39.4 %collective-permute-start.11 = (bf16[112,16,128]{2,1,0:T(8,128)(2,1)}, bf16[112,16,128]{2,1,0:T(8,128)(2,1)}, u32[]{:S(2)}, u32[]{:S(2)}) collective-permute-start(bf16[112,16,128]{2,1,0:T(8,128)(2,1)} %bitcast.7), channel_id=1, source_target_pairs={{0,1},{1,0},{2,3},{3,2},{4,5},{5,4},{6,7},{7,6},{8,9},{9,8},{10,11... | collective-permute-start | bytes 1376264 | tf_op jit(solution)/shard_map/ppermute | solution.py:272
  148.0 29.6 %copy-start = (f32[2,512,512]{2,1,0:T(8,128)S(1)}, f32[2,512,512]{2,1,0:T(8,128)}, u32[]{:S(2)}) copy-start(f32[2,512,512]{2,1,0:T(8,128)} %center.3) | copy-start | bytes 6291460
  150.2 27.4 %collective-permute-start.9 = (bf16[2,192,512]{2,1,0:T(8,128)(2,1)}, bf16[2,192,512]{2,1,0:T(8,128)(2,1)}, u32[]{:S(2)}, u32[]{:S(2)}) collective-permute-start(bf16[2,192,512]{2,1,0:T(8,128)(2,1)} %add_convert_fusion), channel_id=1, source_target_pairs={{32,0},{64,32},{96,64},{128,96},{160,128},{192,160},{224,192},{33,... | collective-permute-start | bytes 1179656 | tf_op jit(solution)/shard_map/ppermute | solution.py:250
  152.8 24.8 %copy-start.4 = (bf16[2,896,256]{2,1,0:T(8,128)(2,1)S(1)}, bf16[2,896,256]{2,1,0:T(8,128)(2,1)}, u32[]{:S(2)}) copy-start(bf16[2,896,256]{2,1,0:T(8,128)(2,1)} %copy-done.3) | copy-start | bytes 2752516
  (7 other events, 44.8 us)

commit v2 on v1

--- a/solution.py
+++ b/solution.py
@@ -24,6 +24,7 @@
 CANVAS = 1280
 TILES = 224
 STEP = 32
+BAND = 96
 F32 = jnp.float32
 BF16 = jnp.bfloat16
 
@@ -64,12 +65,15 @@
 
 
 def illumination_kernel(place, positions, counts, probe, out, canvas, power):
-    for k in range(PS // STEP):
-        rows = pl.ds(k * STEP, STEP)
-        power[rows, :] = probe[0, rows, :] * probe[0, rows, :] + probe[1, rows, :] * probe[1, rows, :]
-    for j in range(CANVAS // 128):
+    power[0] = jnp.zeros((PS, 128), F32)
+    power[4] = jnp.zeros((PS, 128), F32)
+    for j in range(3):
+        cols = pl.ds(j * 128, 128)
+        power[j + 1] = probe[0, :, cols] * probe[0, :, cols] + probe[1, :, cols] * probe[1, :, cols]
+    first, last = PS // 128, (PS + TW) // 128
+    for j in range(first, last):
         canvas[j, pl.ds(PS, TH), :] = jnp.zeros((TH, 128), F32)
-    lanes = lax.broadcasted_iota(jnp.int32, (STEP, 128), 1)
+    lanes = lax.broadcasted_iota(jnp.int32, (BAND, 128), 1)
     grid_r, grid_c = 8, 32
 
     def tile(k, carry):
@@ -88,15 +92,20 @@
             @pl.when(meets)
             def _():
                 block, shift = lane_parts(left)
-
-                def chunk(c, deep):
-                    rows = pl.ds(pl.multiple_of(c * STEP, STEP), STEP)
-                    parts = rolled_out([power[rows, pl.ds(j * 128, 128)] for j in range(3)], shift, lanes)
-                    for j in range(4):
-                        canvas[block + j, pl.ds(top + c * STEP, STEP), :] += parts[j]
-                    return deep
-
-                lax.fori_loop(0, PS // STEP, chunk, 0)
+                low = jnp.maximum(PS - top, 0) // BAND
+                high = (jnp.minimum(PS + TH - top, PS) + BAND - 1) // BAND
+
+                def column(j, wide):
+                    def band(c, deep):
+                        rows = pl.ds(pl.multiple_of(c * BAND, BAND), BAND)
+                        here = pltpu.roll(power[j - block + 1, rows, :], shift, axis=1)
+                        past = pltpu.roll(power[j - block, rows, :], shift, axis=1)
+                        canvas[j, pl.ds(top + c * BAND, BAND), :] += jnp.where(lanes >= shift, here, past)
+                        return deep
+
+                    return lax.fori_loop(low, high, band, wide)
+
+                lax.fori_loop(jnp.maximum(block, first), jnp.minimum(block + 4, last), column, 0)
 
             return inner
 
@@ -105,13 +114,13 @@
     lax.fori_loop(0, 9, tile, 0)
     floor = OBJECT_REG * jnp.max(power[...])
     for j in range(TW // 128):
-        out[:, pl.ds(j * 128, 128)] = 1.0 / (canvas[PS // 128 + j, pl.ds(PS, TH), :] + floor)
+        out[:, pl.ds(j * 128, 128)] = 1.0 / (canvas[first + j, pl.ds(PS, TH), :] + floor)
 
 
 def main_kernel(
     place, positions, counts, center, above, below, before, after, corners_before, corners_after,
     probe, intensity, forward, adjoint,
-    field, rim_before, rim_after, rim_above, rim_below, sums,
+    field, rim_before, rim_after, rim_above, rim_below, kept, given,
     extended, total, wave, halfway, residual, returning, gradient, window, probe_sum,
 ):
     slots = place[0] * 32 + place[1]
@@ -191,13 +200,18 @@
             else:
                 rim = rim_before if j < 2 else rim_after
                 rim[p, :, pl.ds(j % 2 * 128, 128)] = total[p, j].astype(BF16)
-    at = 0
-    for p in range(3):
-        for k in range(PS // 16):
-            for j in range(3):
-                sums[at] = probe_sum[p, pl.ds(k * 16, 16), pl.ds(j * 128, 128)].astype(BF16)
-                at += 1
-    sums[pl.ds(at, TILES - at)] = jnp.zeros((TILES - at, 16, 128), BF16)
+    for core in range(2):
+
+        @pl.when(place[1] % 2 == core)
+        def _():
+            for ref, half, kind in ((kept, core, F32), (given, 1 - core, BF16)):
+                for at in range(TILES // 2):
+                    found = half * (TILES // 2) + at
+                    if found < 216:
+                        p, k, j = found // 72, found // 3 % 24, found % 3
+                        ref[at] = probe_sum[p, pl.ds(k * 16, 16), pl.ds(j * 128, 128)].astype(kind)
+                    else:
+                        ref[at] = jnp.zeros((16, 128), kind)
 
 
 def object_kernel(center, field, from_before, from_after, from_above, from_below, weight, out):
@@ -215,7 +229,10 @@
             out[p, rows, :] = center[p, rows, :] - cells * weight[rows, :]
 
 
-def probe_kernel(sums, probe, out, planes):
+def probe_kernel(place, half, other, probe, out, sums, planes):
+    core = place[1] % 2
+    sums[pl.ds(core * (TILES // 2), TILES // 2)] = half[...]
+    sums[pl.ds((1 - core) * (TILES // 2), TILES // 2)] = other[...]
     at = 0
     for p in range(3):
         for k in range(PS // 16):
@@ -250,29 +267,6 @@
     return lax.ppermute(value, axis, [(k, k + step) for k in range(low, high)])
 
 
-def summed_everywhere(sums):
-    core = lax.axis_index("col") % 2
-    cols = lax.axis_size("col")
-    groups = [list(range(c, cols, 2)) for c in range(2)]
-    members = cols // 2
-    partner = [(k, k ^ 1) for k in range(cols)]
-    halves = sums.reshape(2, TILES // 2, 16, 128)
-    kept = lax.dynamic_index_in_dim(halves, core, 0, keepdims=False)
-    given = lax.dynamic_index_in_dim(halves, 1 - core, 0, keepdims=False)
-    mine = (kept.astype(F32) + lax.ppermute(given, "col", partner).astype(F32)).astype(BF16)
-    mine = mine.reshape(members, -1, 16, 128)
-    parts = lax.all_to_all(mine, "col", 0, 0, axis_index_groups=groups)
-    piece = jnp.sum(parts.astype(F32), axis=0).astype(BF16)
-    rows = lax.axis_size("row")
-    parts = lax.all_to_all(jnp.broadcast_to(piece[None], (rows,) + piece.shape), "row", 0, 0)
-    piece = jnp.sum(parts.astype(F32), axis=0).astype(BF16)
-    half = lax.all_to_all(
-        jnp.broadcast_to(piece[None], (members,) + piece.shape), "col", 0, 0, axis_index_groups=groups
-    ).reshape(TILES // 2, 16, 128)
-    other = lax.ppermute(half, "col", partner)
-    return jnp.where(core == 0, jnp.concatenate([half, other]), jnp.concatenate([other, half]))
-
-
 def on_device(object_field, probe_field, intensities, positions, tile_counts):
     place = jnp.stack([lax.axis_index("row"), lax.axis_index("col")]).astype(jnp.int32)
     where = positions.reshape(-1)
@@ -288,7 +282,7 @@
         out_shape=jax.ShapeDtypeStruct((TH, TW), F32),
         in_specs=[SMEM, SMEM, SMEM, VMEM],
         out_specs=VMEM,
-        scratch_shapes=[pltpu.VMEM((CANVAS // 128, CANVAS, 128), F32), pltpu.VMEM((PS, PS), F32)],
+        scratch_shapes=[pltpu.VMEM((CANVAS // 128, CANVAS, 128), F32), pltpu.VMEM((5, PS, 128), F32)],
         compiler_params=params(24),
         cost_estimate=pl.CostEstimate(flops=20_000_000, bytes_accessed=20_000_000, transcendentals=0),
         name="illumination",
@@ -296,8 +290,9 @@
     corners = jnp.concatenate([above, below], axis=1)
     corners_before = shifted(corners[:, :, TW - 256 :], "col", 1)
     corners_after = shifted(corners[:, :, :256], "col", -1)
+    corners_before, corners_after, weight = lax.optimization_barrier((corners_before, corners_after, weight))
     like = jax.ShapeDtypeStruct
-    field, rim_before, rim_after, rim_above, rim_below, sums = pl.pallas_call(
+    field, rim_before, rim_after, rim_above, rim_below, kept, given = pl.pallas_call(
         main_kernel,
         out_shape=(
             like((2, TH, TW), F32),
@@ -305,10 +300,11 @@
             like((2, EH, 256), BF16),
             like((2, HALF, TW), F32),
             like((2, HALF, TW), F32),
-            like((TILES, 16, 128), BF16),
+            like((TILES // 2, 16, 128), F32),
+            like((TILES // 2, 16, 128), BF16),
         ),
         in_specs=[SMEM] * 3 + [VMEM] * 11,
-        out_specs=(VMEM,) * 6,
+        out_specs=(VMEM,) * 7,
         scratch_shapes=[
             pltpu.VMEM((2, EW // 128, EH, 128), F32),
             pltpu.VMEM((2, EW // 128, EH, 128), F32),
@@ -326,13 +322,27 @@
         place, where, counts, object_field, above, below, before, after, corners_before, corners_after,
         probe_field, intensities.reshape(PMAX, PS, PS), jnp.asarray(forward), jnp.asarray(adjoint),
     )
+    core = place[1] % 2
+    cols, rows = lax.axis_size("col"), lax.axis_size("row")
+    groups = [list(range(c, cols, 2)) for c in range(2)]
+    members = cols // 2
+    partner = [(k, k ^ 1) for k in range(cols)]
+    arrived = lax.ppermute(given, "col", partner)
     from_before = shifted(rim_after, "col", 1)
     from_after = shifted(rim_before, "col", -1)
+    mine = (kept + arrived.astype(F32)).astype(BF16).reshape(members, -1, 16, 128)
+    parts = lax.all_to_all(mine, "col", 0, 0, axis_index_groups=groups)
     up = rim_above + jnp.concatenate([from_before[:, :HALF], from_after[:, :HALF]], axis=2).astype(F32)
     down = rim_below + jnp.concatenate([from_before[:, HALF + TH :], from_after[:, HALF + TH :]], axis=2).astype(F32)
-    from_below = shifted(up.astype(BF16), "row", -1)
-    from_above = shifted(down.astype(BF16), "row", 1)
-    everywhere = summed_everywhere(sums)
+    parts, up, down = lax.optimization_barrier((parts, up.astype(BF16), down.astype(BF16)))
+    from_below = shifted(up, "row", -1)
+    from_above = shifted(down, "row", 1)
+    piece = jnp.sum(parts.astype(F32), axis=0).astype(BF16)
+    parts = lax.all_to_all(jnp.broadcast_to(piece[None], (rows,) + piece.shape), "row", 0, 0)
+    piece = jnp.sum(parts.astype(F32), axis=0).astype(BF16)
+    half = lax.all_to_all(
+        jnp.broadcast_to(piece[None], (members,) + piece.shape), "col", 0, 0, axis_index_groups=groups
+    ).reshape(TILES // 2, 16, 128)
     new_object = pl.pallas_call(
         object_kernel,
         out_shape=like((2, TH, TW), F32),
@@ -342,15 +352,17 @@
         cost_estimate=pl.CostEstimate(flops=4_000_000, bytes_accessed=12_000_000, transcendentals=0),
         name="new_object",
     )(object_field, field, from_before, from_after, from_above, from_below, weight)
+    half, new_object = lax.optimization_barrier((half, new_object))
+    other = lax.ppermute(half, "col", partner)
     new_probe = pl.pallas_call(
         probe_kernel,
         out_shape=like((2, PS, PS), F32),
-        in_specs=[VMEM] * 2,
+        in_specs=[SMEM, VMEM, VMEM, VMEM],
         out_specs=VMEM,
-        scratch_shapes=[pltpu.VMEM((3, PS, PS), F32)],
+        scratch_shapes=[pltpu.VMEM((TILES, 16, 128), BF16), pltpu.VMEM((3, PS, PS), F32)],
         compiler_params=params(24),
         name="new_probe",
-    )(everywhere, probe_field)
+    )(place, half, other, probe_field)
     return (new_object, new_probe)
 
 

time: 187 us -> 185 us (0.989)
  waiting for transfers between devices: 47.9 us -> 53.2 us
  other arithmetic: 10.2 us -> 5.05 us
  starting transfers between devices: 74.2 us -> 70.9 us
  local copies, waits for them, and re-layouts: 9.52 us -> 11.4 us
    unnamed x36 -> x44, local copies, waits for them, and re-layouts: 3.31 us -> 8.18 us
    convert_element_type x3 -> x2, other arithmetic: 6.17 us -> 3.14 us  [the longest x1 2.11 us: on_device(): (kept + arrived.astype(F32)).astype(BF16).reshape(members, -1, 16, 128)]
    all_to_all x2, waiting for transfers between devices: 7.35 us -> 9.76 us  [the longest x1 9.76 us: on_device(): parts = lax.all_to_all(mine, 'col', 0, 0, axis_index_groups=groups)]
    ppermute x2, starting transfers between devices: 5.26 us -> 3.19 us  [the longest x1 2.36 us: on_device(): other = lax.ppermute(half, 'col', partner)]
    pallas_call x1, Pallas kernels: 8.13 us -> 6.17 us  [on_device(): pl.pallas_call(illumination_kernel, out_shape=jax.ShapeDtypeStruct((TH, T...]
  transfers between devices with their start and end apart: 14 -> 14, of which waited for: 8 -> 7; matrix products, arithmetic and copies ran while one was open for 6% -> 3% of each run, Pallas kernels for 6% -> 4%
where the time goes in v2:
time: 185 us; the launch traced here: 184 us
  starting transfers between devices  70.9 us (38%)
  waiting for transfers between devices  53.2 us (29%)
  Pallas kernels  30.2 us (16%)
  blocking collectives  12.7 us (7%)
  local copies, waits for them, and re-layouts  11.4 us (6%)
  other arithmetic  5.05 us (3%)
    ppermute x10, waiting for transfers between devices, shifted(): return lax.ppermute(value, axis, [(k, k + step) for k in range(low, high)])  41 us
    ppermute x10, starting transfers between devices, shifted(): return lax.ppermute(value, axis, [(k, k + step) for k in range(low, high)])  36.7 us
    all_to_all x1, starting transfers between devices, on_device(): parts = lax.all_to_all(mine, 'col', 0, 0, axis_index_groups=groups)  26.7 us
    pallas_call x1, Pallas kernels, on_device(): pl.pallas_call(main_kernel, out_shape=(like((2, TH, TW), F32), like((2, E...  19.4 us
    all_to_all x1, blocking collectives, on_device(): lax.all_to_all(jnp.broadcast_to(piece[None], (rows,) + piece.shape), 'row...  12.7 us
    all_to_all x1, waiting for transfers between devices, on_device(): parts = lax.all_to_all(mine, 'col', 0, 0, axis_index_groups=groups)  9.76 us
    unnamed x44, local copies, waits for them, and re-layouts  8.18 us
    pallas_call x1, Pallas kernels, on_device(): pl.pallas_call(illumination_kernel, out_shape=jax.ShapeDtypeStruct((TH, T...  6.17 us
  transfers between devices with their start and end apart: 14, of which 7 were waited for; matrix products, arithmetic and copies ran while one was open for 3% of the time, Pallas kernels for 4%

profile of v2, /device:TPU:57, one launch (start us, length us, event | category | flops | bytes accessed | tf_op | source)
XLA Modules:
  0.0 184.4 jit_solution(858046059118813542)
XLA Ops:
  0.6 1.7 convert_element_type.25
  2.4 7.6 %collective-permute-start = (bf16[2,192,512]{2,1,0:T(8,128)(2,1)S(1)}, bf16[2,192,512]{2,1,0:T(8,128)(2,1)S(1)}, u32[]{:S(2)}, u32[]{:S(2)}) collective-permute-start(bf16[2,192,512]{2,1,0:T(8,128)(2,1)S(1)} %get-tuple-element.35), channel_id=1, source_target_pairs={{0,32},{32,64},{64,96},{96,128},{128,160},{160,192},{192,224},{1,3... | collective-permute-start | bytes 1179656 | tf_op jit(solution)/shard_map/ppermute | solution.py:267
  10.0 1.9 %collective-permute-start.1 = (bf16[2,192,512]{2,1,0:T(8,128)(2,1)S(1)}, bf16[2,192,512]{2,1,0:T(8,128)(2,1)S(1)}, u32[]{:S(2)}, u32[]{:S(2)}) collective-permute-start(bf16[2,192,512]{2,1,0:T(8,128)(2,1)S(1)} %get-tuple-element.34), channel_id=1, source_target_pairs={{32,0},{64,32},{96,64},{128,96},{160,128},{192,160},{224,192},{33,... | collective-permute-start | bytes 1179656 | tf_op jit(solution)/shard_map/ppermute | solution.py:267
  13.0 3.0 %collective-permute-start.3 = (bf16[2,512,256]{2,1,0:T(8,128)(2,1)}, bf16[2,512,256]{2,1,0:T(8,128)(2,1)}, u32[]{:S(2)}, u32[]{:S(2)}) collective-permute-start(bf16[2,512,256]{2,1,0:T(8,128)(2,1)} %get-tuple-element.32), channel_id=1, source_target_pairs={{1,0},{2,1},{3,2},{4,3},{5,4},{6,5},{7,6},{8,7},{9,8},{10,9},{11,1... | collective-permute-start | bytes 1572872 | tf_op jit(solution)/shard_map/ppermute | solution.py:267
  16.0 3.0 %collective-permute-start.2 = (bf16[2,512,256]{2,1,0:T(8,128)(2,1)}, bf16[2,512,256]{2,1,0:T(8,128)(2,1)}, u32[]{:S(2)}, u32[]{:S(2)}) collective-permute-start(bf16[2,512,256]{2,1,0:T(8,128)(2,1)} %get-tuple-element.33), channel_id=1, source_target_pairs={{0,1},{1,2},{2,3},{3,4},{4,5},{5,6},{6,7},{7,8},{8,9},{9,10},{10,1... | collective-permute-start | bytes 1572872 | tf_op jit(solution)/shard_map/ppermute | solution.py:267
  19.0 7.3 %collective-permute-done.above = bf16[2,192,512]{2,1,0:T(8,128)(2,1)S(1)} collective-permute-done((bf16[2,192,512]{2,1,0:T(8,128)(2,1)S(1)}, bf16[2,192,512]{2,1,0:T(8,128)(2,1)S(1)}, u32[]{:S(2)}, u32[]{:S(2)}) %collective-permute-start) | collective-permute-done | bytes 393248 | tf_op jit(solution)/shard_map/ppermute | solution.py:267
  26.4 10.1 %collective-permute-done.1.below = bf16[2,192,512]{2,1,0:T(8,128)(2,1)S(1)} collective-permute-done((bf16[2,192,512]{2,1,0:T(8,128)(2,1)S(1)}, bf16[2,192,512]{2,1,0:T(8,128)(2,1)S(1)}, u32[]{:S(2)}, u32[]{:S(2)}) %collective-permute-start.1) | collective-permute-done | bytes 393248 | tf_op jit(solution)/shard_map/ppermute | solution.py:267
  37.3 3.5 %collective-permute-start.5 = (bf16[2,384,256]{2,1,0:T(8,128)(2,1)}, bf16[2,384,256]{2,1,0:T(8,128)(2,1)}, u32[]{:S(2)}, u32[]{:S(2)}) collective-permute-start(bf16[2,384,256]{2,1,0:T(8,128)(2,1)} %get-tuple-element.40), channel_id=1, source_target_pairs={{1,0},{2,1},{3,2},{4,3},{5,4},{6,5},{7,6},{8,7},{9,8},{10,9},{11,1... | collective-permute-start | bytes 1179656 | tf_op jit(solution)/shard_map/ppermute | solution.py:267
  40.7 2.9 %collective-permute-start.4 = (bf16[2,384,256]{2,1,0:T(8,128)(2,1)S(1)}, bf16[2,384,256]{2,1,0:T(8,128)(2,1)}, u32[]{:S(2)}, u32[]{:S(2)}) collective-permute-start(bf16[2,384,256]{2,1,0:T(8,128)(2,1)S(1)} %get-tuple-element.41), channel_id=1, source_target_pairs={{0,1},{1,2},{2,3},{3,4},{4,5},{5,6},{6,7},{7,8},{8,9},{9,10},{10,1... | collective-permute-start | bytes 1179656 | tf_op jit(solution)/shard_map/ppermute | solution.py:267
  44.6 6.2 %illumination.1.weight = f32[512,512]{1,0:T(8,128)S(1)} custom-call(s32[2]{0:T(128)S(1)} %pad_add_fusion.place, s32[3072]{0:T(1024)S(1)} %reshape.21.positions, s32[256]{0:T(256)S(1)} %reshape.22.counts, f32[2,384,384]{2,1,0:T(8,128)S(1)} %copy-done.1), custom_call_target="tpu_custom_call" | custom-call | flops 20000000 | bytes 20000000 | tf_op jit(solution)/shard_map/illumination/pallas_call | solution.py:280
  51.8 19.4 %slots.1 = (f32[2,512,512]{2,1,0:T(8,128)}, bf16[2,896,256]{2,1,0:T(8,128)(2,1)}, bf16[2,896,256]{2,1,0:T(8,128)(2,1)}, f32[2,192,512]{2,1,0:T(8,128)}, f32[2,19...) custom-call(s32[2]{0:T(128)} %copy-done.12, s32[3072]{0:T(1024)} %copy-done.10, ...), custom_call_target="tpu_custom_call" | custom-call | tf_op jit(solution)/shard_map/slots/pallas_call | solution.py:295
  71.2 7.3 %collective-permute-start.7 = (bf16[2,896,256]{2,1,0:T(8,128)(2,1)}, bf16[2,896,256]{2,1,0:T(8,128)(2,1)S(1)}, u32[]{:S(2)}, u32[]{:S(2)}) collective-permute-start(bf16[2,896,256]{2,1,0:T(8,128)(2,1)} %get-tuple-element.22), channel_id=1, source_target_pairs={{0,1},{1,2},{2,3},{3,4},{4,5},{5,6},{6,7},{7,8},{8,9},{9,10},{10,1... | collective-permute-start | bytes 2752520 | tf_op jit(solution)/shard_map/ppermute | solution.py:267
  79.4 1.9 %collective-permute-start.8 = (bf16[2,896,256]{2,1,0:T(8,128)(2,1)}, bf16[2,896,256]{2,1,0:T(8,128)(2,1)S(1)}, u32[]{:S(2)}, u32[]{:S(2)}) collective-permute-start(bf16[2,896,256]{2,1,0:T(8,128)(2,1)} %get-tuple-element.23), channel_id=1, source_target_pairs={{1,0},{2,1},{3,2},{4,3},{5,4},{6,5},{7,6},{8,7},{9,8},{10,9},{11,1... | collective-permute-start | bytes 2752520 | tf_op jit(solution)/shard_map/ppermute | solution.py:267
  82.1 2.1 %add_convert_fusion = bf16[112,16,128]{2,1,0:T(8,128)(2,1)} fusion(f32[112,16,128]{2,1,0:T(8,128)} %get-tuple-element.19, bf16[112,16,128]{2,1,0:T(8,128)(2,1)S(1)} %collective-permute-done.6), kind=kLoop, calls=%fused_computation | loop fusion | flops 688128 | bytes 1835008 | tf_op jit(solution)/shard_map/convert_element_type | solution.py:333
  84.2 26.7 %all-to-all-start = ((bf16[16,7,16,128]{3,2,1,0:T(8,128)(2,1)}), bf16[16,7,16,128]{3,2,1,0:T(8,128)(2,1)S(1)}, u32[]{:S(2)}, u32[]{:S(2)}) async-start(bf16[16,7,16,128]{3,2,1,0:T(8,128)(2,1)} %bitcast.3), calls=%async_computation | async-start | bytes 917504 | tf_op jit(solution)/shard_map/all_to_all | solution.py:334
  113.6 9.8 %all-to-all-done = bf16[16,7,16,128]{3,2,1,0:T(8,128)(2,1)S(1)} async-done(((bf16[16,7,16,128]{3,2,1,0:T(8,128)(2,1)}), bf16[16,7,16,128]{3,2,1,0:T(8,128)(2,1)S(1)}, u32[]{:S(2)}, u32[]{:S(2)}) %all-to-all-start) | async-done | bytes 458784 | tf_op jit(solution)/shard_map/all_to_all | solution.py:334
  123.5 12.7 %all_to_all.15 = bf16[8,7,16,128]{3,2,1,0:T(8,128)(2,1)S(1)} all-to-all(bf16[8,7,16,128]{3,2,1,0:T(8,128)(2,1)S(1)} %broadcast_in_dim.4), channel_id=1, replica_groups=mesh['row'=8,'col'=32] {'row'}, dimensions={0} | all-to-all | bytes 458752 | tf_op jit(solution)/shard_map/all_to_all | solution.py:341
  137.1 4.3 %all-to-all-start.2 = ((bf16[16,7,16,128]{3,2,1,0:T(8,128)(2,1)}), bf16[16,7,16,128]{3,2,1,0:T(8,128)(2,1)}, u32[]{:S(2)}, u32[]{:S(2)}) async-start(bf16[16,7,16,128]{3,2,1,0:T(8,128)(2,1)} %broadcast_in_dim.5), calls=%async_computation.2 | async-start | bytes 917504 | tf_op jit(solution)/shard_map/all_to_all | solution.py:343
  141.4 3.7 %collective-permute-start.9 = (bf16[2,192,512]{2,1,0:T(8,128)(2,1)S(1)}, bf16[2,192,512]{2,1,0:T(8,128)(2,1)S(1)}, u32[]{:S(2)}, u32[]{:S(2)}) collective-permute-start(bf16[2,192,512]{2,1,0:T(8,128)(2,1)S(1)} %get-tuple-element.27), channel_id=1, source_target_pairs={{0,32},{32,64},{64,96},{96,128},{128,160},{160,192},{192,224},{1,3... | collective-permute-start | bytes 1179656 | tf_op jit(solution)/shard_map/ppermute | solution.py:267
  145.1 1.9 %collective-permute-start.10 = (bf16[2,192,512]{2,1,0:T(8,128)(2,1)S(1)}, bf16[2,192,512]{2,1,0:T(8,128)(2,1)S(1)}, u32[]{:S(2)}, u32[]{:S(2)}) collective-permute-start(bf16[2,192,512]{2,1,0:T(8,128)(2,1)S(1)} %copy-done.18), channel_id=1, source_target_pairs={{32,0},{64,32},{96,64},{128,96},{160,128},{192,160},{224,192},{33,... | collective-permute-start | bytes 1179656 | tf_op jit(solution)/shard_map/ppermute | solution.py:267
  147.0 18.9 %collective-permute-done.9.from_above = bf16[2,192,512]{2,1,0:T(8,128)(2,1)S(1)} collective-permute-done((bf16[2,192,512]{2,1,0:T(8,128)(2,1)S(1)}, bf16[2,192,512]{2,1,0:T(8,128)(2,1)S(1)}, u32[]{:S(2)}, u32[]{:S(2)}) %collective-permute-start.9) | collective-permute-done | bytes 393248 | tf_op jit(solution)/shard_map/ppermute | solution.py:267
  166.0 4.6 %collective-permute-done.10.from_below = bf16[2,192,512]{2,1,0:T(8,128)(2,1)S(1)} collective-permute-done((bf16[2,192,512]{2,1,0:T(8,128)(2,1)S(1)}, bf16[2,192,512]{2,1,0:T(8,128)(2,1)S(1)}, u32[]{:S(2)}, u32[]{:S(2)}) %collective-permute-start.10) | collective-permute-done | bytes 393248 | tf_op jit(solution)/shard_map/ppermute | solution.py:267
  177.5 2.4 %collective-permute-start.11 = (bf16[112,16,128]{2,1,0:T(8,128)(2,1)}, bf16[112,16,128]{2,1,0:T(8,128)(2,1)S(1)}, u32[]{:S(2)}, u32[]{:S(2)}) collective-permute-start(bf16[112,16,128]{2,1,0:T(8,128)(2,1)} %bitcast.4.half), channel_id=1, source_target_pairs={{0,1},{1,0},{2,3},{3,2},{4,5},{5,4},{6,7},{7,6},{8,9},{9,8},{10,11... | collective-permute-start | bytes 1376264 | tf_op jit(solution)/shard_map/ppermute | solution.py:356
  181.5 2.9 %new_probe.1 = f32[2,384,384]{2,1,0:T(8,128)} custom-call(s32[2]{0:T(128)S(1)} %copy-done.13, bf16[112,16,128]{2,1,0:T(8,128)(2,1)} %bitcast.4.half, bf16[112,16,128]{2,1,0:T(8,128)(2,1)S(1)} %collective-permute-done.11.other, f32[2,384,384]{2,1,0:T(8,128)S(1)} %copy-done.2), custom_call_target="tpu_custom_call" | custom-call | tf_op jit(solution)/shard_map/new_probe/pallas_call | solution.py:357
  (69 shorter events, 17.6 us)
Async XLA Ops:
  2.4 23.9 %collective-permute-start = (bf16[2,192,512]{2,1,0:T(8,128)(2,1)S(1)}, bf16[2,192,512]{2,1,0:T(8,128)(2,1)S(1)}, u32[]{:S(2)}, u32[]{:S(2)}) collective-permute-start(bf16[2,192,512]{2,1,0:T(8,128)(2,1)S(1)} %get-tuple-element.35), channel_id=1, source_target_pairs={{0,32},{32,64},{64,96},{96,128},{128,160},{160,192},{192,224},{1,3... | collective-permute-start | bytes 1179656 | tf_op jit(solution)/shard_map/ppermute | solution.py:267
  10.0 26.4 %collective-permute-start.1 = (bf16[2,192,512]{2,1,0:T(8,128)(2,1)S(1)}, bf16[2,192,512]{2,1,0:T(8,128)(2,1)S(1)}, u32[]{:S(2)}, u32[]{:S(2)}) collective-permute-start(bf16[2,192,512]{2,1,0:T(8,128)(2,1)S(1)} %get-tuple-element.34), channel_id=1, source_target_pairs={{32,0},{64,32},{96,64},{128,96},{160,128},{192,160},{224,192},{33,... | collective-permute-start | bytes 1179656 | tf_op jit(solution)/shard_map/ppermute | solution.py:267
  13.0 30.7 %copy-start.20 = (s32[8,32]{1,0:T(8,128)S(1)}, s32[8,32]{1,0:T(8,128)}, u32[]{:S(2)}) copy-start(s32[8,32]{1,0:T(8,128)} %param.11) | copy-start | bytes 3076
  13.0 30.8 %copy-start.19 = (s32[8,32,6,2]{1,3,2,0:T(2,128)S(1)}, s32[8,32,6,2]{1,3,2,0:T(2,128)}, u32[]{:S(2)}) copy-start(s32[8,32,6,2]{1,3,2,0:T(2,128)} %param.10) | copy-start | bytes 36868
  13.0 38.8 %collective-permute-start.3 = (bf16[2,512,256]{2,1,0:T(8,128)(2,1)}, bf16[2,512,256]{2,1,0:T(8,128)(2,1)}, u32[]{:S(2)}, u32[]{:S(2)}) collective-permute-start(bf16[2,512,256]{2,1,0:T(8,128)(2,1)} %get-tuple-element.32), channel_id=1, source_target_pairs={{1,0},{2,1},{3,2},{4,3},{5,4},{6,5},{7,6},{8,7},{9,8},{10,9},{11,1... | collective-permute-start | bytes 1572872 | tf_op jit(solution)/shard_map/ppermute | solution.py:267
  16.0 35.8 %collective-permute-start.2 = (bf16[2,512,256]{2,1,0:T(8,128)(2,1)}, bf16[2,512,256]{2,1,0:T(8,128)(2,1)}, u32[]{:S(2)}, u32[]{:S(2)}) collective-permute-start(bf16[2,512,256]{2,1,0:T(8,128)(2,1)} %get-tuple-element.33), channel_id=1, source_target_pairs={{0,1},{1,2},{2,3},{3,4},{4,5},{5,6},{6,7},{7,8},{8,9},{9,10},{10,1... | collective-permute-start | bytes 1572872 | tf_op jit(solution)/shard_map/ppermute | solution.py:267
  26.3 17.9 %copy-start.14 = (bf16[2,192,512]{2,1,0:T(8,128)(2,1)}, bf16[2,192,512]{2,1,0:T(8,128)(2,1)S(1)}, u32[]{:S(2)}) copy-start(bf16[2,192,512]{2,1,0:T(8,128)(2,1)S(1)} %collective-permute-done.above) | copy-start | bytes 1179652
  36.4 8.1 %copy-start.15 = (bf16[2,192,512]{2,1,0:T(8,128)(2,1)}, bf16[2,192,512]{2,1,0:T(8,128)(2,1)S(1)}, u32[]{:S(2)}) copy-start(bf16[2,192,512]{2,1,0:T(8,128)(2,1)S(1)} %collective-permute-done.1.below) | copy-start | bytes 1179652
  36.4 8.1 %copy-start.1 = (f32[2,384,384]{2,1,0:T(8,128)S(1)}, f32[2,384,384]{2,1,0:T(8,128)}, u32[]{:S(2)}) copy-start(f32[2,384,384]{2,1,0:T(8,128)} %probe.5) | copy-start | bytes 3538948
  37.3 14.5 %collective-permute-start.5 = (bf16[2,384,256]{2,1,0:T(8,128)(2,1)}, bf16[2,384,256]{2,1,0:T(8,128)(2,1)}, u32[]{:S(2)}, u32[]{:S(2)}) collective-permute-start(bf16[2,384,256]{2,1,0:T(8,128)(2,1)} %get-tuple-element.40), channel_id=1, source_target_pairs={{1,0},{2,1},{3,2},{4,3},{5,4},{6,5},{7,6},{8,7},{9,8},{10,9},{11,1... | collective-permute-start | bytes 1179656 | tf_op jit(solution)/shard_map/ppermute | solution.py:267
  40.7 11.0 %collective-permute-start.4 = (bf16[2,384,256]{2,1,0:T(8,128)(2,1)S(1)}, bf16[2,384,256]{2,1,0:T(8,128)(2,1)}, u32[]{:S(2)}, u32[]{:S(2)}) collective-permute-start(bf16[2,384,256]{2,1,0:T(8,128)(2,1)S(1)} %get-tuple-element.41), channel_id=1, source_target_pairs={{0,1},{1,2},{2,3},{3,4},{4,5},{5,6},{6,7},{7,8},{8,9},{9,10},{10,1... | collective-permute-start | bytes 1179656 | tf_op jit(solution)/shard_map/ppermute | solution.py:267
  44.5 7.3 %copy-start.10 = (s32[3072]{0:T(1024)}, s32[3072]{0:T(1024)S(1)}, u32[]{:S(2)}) copy-start(s32[3072]{0:T(1024)S(1)} %reshape.21.positions) | copy-start | bytes 36868
  44.6 7.2 %copy-start.12 = (s32[2]{0:T(128)}, s32[2]{0:T(128)S(1)}, u32[]{:S(2)}) copy-start(s32[2]{0:T(128)S(1)} %pad_add_fusion.place) | copy-start | bytes 28
  71.2 39.7 %collective-permute-start.7 = (bf16[2,896,256]{2,1,0:T(8,128)(2,1)}, bf16[2,896,256]{2,1,0:T(8,128)(2,1)S(1)}, u32[]{:S(2)}, u32[]{:S(2)}) collective-permute-start(bf16[2,896,256]{2,1,0:T(8,128)(2,1)} %get-tuple-element.22), channel_id=1, source_target_pairs={{0,1},{1,2},{2,3},{3,4},{4,5},{5,6},{6,7},{7,8},{8,9},{9,10},{10,1... | collective-permute-start | bytes 2752520 | tf_op jit(solution)/shard_map/ppermute | solution.py:267
  78.5 3.5 %collective-permute-start.6 = (bf16[112,16,128]{2,1,0:T(8,128)(2,1)}, bf16[112,16,128]{2,1,0:T(8,128)(2,1)S(1)}, u32[]{:S(2)}, u32[]{:S(2)}) collective-permute-start(bf16[112,16,128]{2,1,0:T(8,128)(2,1)} %get-tuple-element.20), channel_id=1, source_target_pairs={{0,1},{1,0},{2,3},{3,2},{4,5},{5,4},{6,7},{7,6},{8,9},{9,8},{10,11... | collective-permute-start | bytes 1376264 | tf_op jit(solution)/shard_map/ppermute | solution.py:330
  79.4 31.6 %collective-permute-start.8 = (bf16[2,896,256]{2,1,0:T(8,128)(2,1)}, bf16[2,896,256]{2,1,0:T(8,128)(2,1)S(1)}, u32[]{:S(2)}, u32[]{:S(2)}) collective-permute-start(bf16[2,896,256]{2,1,0:T(8,128)(2,1)} %get-tuple-element.23), channel_id=1, source_target_pairs={{1,0},{2,1},{3,2},{4,3},{5,4},{6,5},{7,6},{8,7},{9,8},{10,9},{11,1... | collective-permute-start | bytes 2752520 | tf_op jit(solution)/shard_map/ppermute | solution.py:267
  82.1 30.1 %copy-start.16 = (f32[2,192,512]{2,1,0:T(8,128)S(1)}, f32[2,192,512]{2,1,0:T(8,128)}, u32[]{:S(2)}) copy-start(f32[2,192,512]{2,1,0:T(8,128)} %get-tuple-element.21) | copy-start | bytes 2359300
  84.2 39.2 %all-to-all-start = ((bf16[16,7,16,128]{3,2,1,0:T(8,128)(2,1)}), bf16[16,7,16,128]{3,2,1,0:T(8,128)(2,1)S(1)}, u32[]{:S(2)}, u32[]{:S(2)}) async-start(bf16[16,7,16,128]{3,2,1,0:T(8,128)(2,1)} %bitcast.3), calls=%async_computation | async-start | bytes 917504 | tf_op jit(solution)/shard_map/all_to_all | solution.py:334
  113.6 31.5 %copy-start.18 = (bf16[2,192,512]{2,1,0:T(8,128)(2,1)S(1)}, bf16[2,192,512]{2,1,0:T(8,128)(2,1)}, u32[]{:S(2)}) copy-start(bf16[2,192,512]{2,1,0:T(8,128)(2,1)} %get-tuple-element.28) | copy-start | bytes 1179652
  113.6 57.0 %copy-start = (f32[2,512,512]{2,1,0:T(8,128)S(1)}, f32[2,512,512]{2,1,0:T(8,128)}, u32[]{:S(2)}) copy-start(f32[2,512,512]{2,1,0:T(8,128)} %center.3) | copy-start | bytes 6291460
  137.1 40.4 %all-to-all-start.2 = ((bf16[16,7,16,128]{3,2,1,0:T(8,128)(2,1)}), bf16[16,7,16,128]{3,2,1,0:T(8,128)(2,1)}, u32[]{:S(2)}, u32[]{:S(2)}) async-start(bf16[16,7,16,128]{3,2,1,0:T(8,128)(2,1)} %broadcast_in_dim.5), calls=%async_computation.2 | async-start | bytes 917504 | tf_op jit(solution)/shard_map/all_to_all | solution.py:343
  141.4 24.6 %collective-permute-start.9 = (bf16[2,192,512]{2,1,0:T(8,128)(2,1)S(1)}, bf16[2,192,512]{2,1,0:T(8,128)(2,1)S(1)}, u32[]{:S(2)}, u32[]{:S(2)}) collective-permute-start(bf16[2,192,512]{2,1,0:T(8,128)(2,1)S(1)} %get-tuple-element.27), channel_id=1, source_target_pairs={{0,32},{32,64},{64,96},{96,128},{128,160},{160,192},{192,224},{1,3... | collective-permute-start | bytes 1179656 | tf_op jit(solution)/shard_map/ppermute | solution.py:267
  145.1 25.5 %collective-permute-start.10 = (bf16[2,192,512]{2,1,0:T(8,128)(2,1)S(1)}, bf16[2,192,512]{2,1,0:T(8,128)(2,1)S(1)}, u32[]{:S(2)}, u32[]{:S(2)}) collective-permute-start(bf16[2,192,512]{2,1,0:T(8,128)(2,1)S(1)} %copy-done.18), channel_id=1, source_target_pairs={{32,0},{64,32},{96,64},{128,96},{160,128},{192,160},{224,192},{33,... | collective-permute-start | bytes 1179656 | tf_op jit(solution)/shard_map/ppermute | solution.py:267
  177.5 4.0 %collective-permute-start.11 = (bf16[112,16,128]{2,1,0:T(8,128)(2,1)}, bf16[112,16,128]{2,1,0:T(8,128)(2,1)S(1)}, u32[]{:S(2)}, u32[]{:S(2)}) collective-permute-start(bf16[112,16,128]{2,1,0:T(8,128)(2,1)} %bitcast.4.half), channel_id=1, source_target_pairs={{0,1},{1,0},{2,3},{3,2},{4,5},{5,4},{6,7},{7,6},{8,9},{9,8},{10,11... | collective-permute-start | bytes 1376264 | tf_op jit(solution)/shard_map/ppermute | solution.py:356
  (11 other events, 28.4 us)
